TPU v7x, 32 devices: a whole 2x2x4 slice. The times are simulated.
32 devices in a mesh: req: 2 (over y), ctx: 16 (over z, x, core).
Axes of the slice: x: 2, y: 2, z: 4, core: 2. Of those that a mesh axis runs over, the one named last changes fastest.
Arguments:
- q_latent: bfloat16 [128, 48, 512], P(None, 'req'), parts along dimension 1, may hold values from -64 to 64
- q_rope: bfloat16 [128, 3072], P(None, 'req'), parts along dimension 1, may hold values from -6 to 6
- cache_latent: bfloat16 [128, 128, 512], P(('req', 'ctx')), parts along dimension 0, may hold values from -6 to 6
- cache_rope: bfloat16 [128, 64, 128], P(('req', 'ctx')), parts along dimension 0, may hold values from -6 to 6
- new_latent: bfloat16 [48, 512], P('req'), parts along dimension 0, may hold values from -6 to 6
- new_rope: bfloat16 [48, 64], P('req'), parts along dimension 0, may hold values from -6 to 6
- removed: int32 [24, 2], P('req'), parts along dimension 0, may hold values from 1 to 63, as said below
Outputs:
- attended: bfloat16 [128, 48, 512], P('ctx', 'req'), parts along dimension 1
There are 2 independent parts, one for each index of `req`. A program takes and returns all parts, laid end to end along the dimension named above; each array names one. Nothing has to cross between parts.
Inputs may be any that keep to these rules, and one draw needn't show every extreme that they name: Each row (first, last) names the blocks first to last - 1 of one removed span of whole blocks. Rows ascend, the spans are disjoint and are parted by at least one kept block; the first span starts at block 1 and the last ends at block 63.
All inputs are finite; a program needn't handle non-finite values.
Results may differ from a plain program's by a relative error of at most 0.0024.
Values may be sent and summed in bfloat16 or wider, within the bound.
A program may use at most 64 MiB of HBM per device.

v0:
```python
import jax
import jax.numpy as jnp
import numpy as np
from jax import lax
from jax.sharding import PartitionSpec as P

floor_value = -1e30
score_scale = 192.0 ** (-0.5)


def rope_tables(rope_width):
    halves = rope_width // 2
    frequencies = 10000.0 ** (-2.0 * np.arange(halves) / rope_width)
    coarse = np.mod(4096.0 * frequencies, 2.0 * np.pi)
    middle = np.mod(64.0 * frequencies, 2.0 * np.pi)
    return (
        jnp.asarray(frequencies, jnp.float32),
        jnp.asarray(coarse, jnp.float32),
        jnp.asarray(middle, jnp.float32),
    )


def turn_angles(shift_rows, rope_width):
    frequencies, coarse, middle = rope_tables(rope_width)
    magnitude = jnp.abs(shift_rows)
    signed = jnp.where(shift_rows < 0, -1.0, 1.0).astype(jnp.float32)
    upper_part = (magnitude // 4096).astype(jnp.float32)[..., None]
    centre_part = (magnitude // 64 % 64).astype(jnp.float32)[..., None]
    lowest_part = (magnitude % 64).astype(jnp.float32)[..., None]
    angles = upper_part * coarse + centre_part * middle + lowest_part * frequencies
    return (jnp.cos(angles), signed[..., None] * jnp.sin(angles))


def rotate_last(values, cosine, sine_part):
    halves = values.shape[-1] // 2
    first_half = values[..., :halves]
    second_half = values[..., halves:]
    return jnp.concatenate(
        [
            first_half * cosine - second_half * sine_part,
            first_half * sine_part + second_half * cosine,
        ],
        axis=-1,
    )


def rotate_middle(values, cosine, sine_part):
    halves = values.shape[1] // 2
    first_half = values[:, :halves, :]
    second_half = values[:, halves:, :]
    return jnp.concatenate(
        [
            first_half * cosine - second_half * sine_part,
            first_half * sine_part + second_half * cosine,
        ],
        axis=1,
    )


def span_info(removed, total_blocks, block_rows):
    starts = removed[:, 0]
    finishes = removed[:, 1]
    block_ids = jnp.arange(total_blocks, dtype=jnp.int32)
    inside = (block_ids[:, None] >= starts[None, :]) & (block_ids[:, None] < finishes[None, :])
    kept_block = jnp.logical_not(jnp.any(inside, axis=1))
    drop_before = block_rows * jnp.sum(
        jnp.clip(block_ids[:, None], starts[None, :], finishes[None, :]) - starts[None, :], axis=1
    )
    kept_rows = total_blocks * block_rows - block_rows * jnp.sum(finishes - starts)
    return (kept_block, drop_before, kept_rows)


def block_terms(query_rows, rope_rows, latent_block, key_block):
    contract = (((1,), (1,)), ((), ()))
    scores = (
        lax.dot_general(query_rows, latent_block, contract, preferred_element_type=jnp.float32)
        + jnp.dot(rope_rows, key_block, preferred_element_type=jnp.float32)
    ) * score_scale
    block_max = jnp.max(scores, axis=1)
    weights = jnp.exp(scores - block_max[:, None]).astype(jnp.bfloat16)
    block_sum = jnp.sum(weights.astype(jnp.float32), axis=1)
    block_out = jnp.dot(weights, latent_block, preferred_element_type=jnp.float32)
    return (block_max, block_sum, block_out)


def absorb(carried, produced, kept_flag):
    run_max, run_sum, run_acc = carried
    block_max, block_sum, block_out = produced
    keep_part = kept_flag.astype(jnp.float32)
    lifted = jnp.where(kept_flag, block_max, floor_value)
    new_max = jnp.maximum(run_max, lifted)
    old_scale = jnp.exp(run_max - new_max)
    add_scale = jnp.exp(lifted - new_max) * keep_part
    return (
        new_max,
        run_sum * old_scale + block_sum * add_scale,
        run_acc * old_scale[:, None] + block_out * add_scale[:, None],
    )


def empty_state(row_total, lat_width):
    return (
        jnp.full((row_total,), floor_value, jnp.float32),
        jnp.zeros((row_total,), jnp.float32),
        jnp.zeros((row_total, lat_width), jnp.float32),
    )


def finish(own_max, own_sum, own_acc, own_rows, own_rope, new_latent, new_keys, tokens):
    row_total = own_rows.shape[0]
    own_max = own_max.reshape(row_total)
    own_sum = own_sum.reshape(row_total)
    own_acc = own_acc.reshape(row_total, new_latent.shape[1])
    contract = (((1,), (1,)), ((), ()))
    new_scores = (
        lax.dot_general(own_rows, new_latent, contract, preferred_element_type=jnp.float32)
        + lax.dot_general(own_rope, new_keys, contract, preferred_element_type=jnp.float32)
    ) * score_scale
    row_token = jnp.arange(row_total, dtype=jnp.int32) % tokens
    causal = jnp.arange(tokens, dtype=jnp.int32)[None, :] <= row_token[:, None]
    masked = jnp.where(causal, new_scores, floor_value)
    new_max = jnp.max(masked, axis=1)
    new_weights = jnp.where(causal, jnp.exp(masked - new_max[:, None]), 0.0).astype(jnp.bfloat16)
    new_sum = jnp.sum(new_weights.astype(jnp.float32), axis=1)
    new_out = jnp.dot(new_weights, new_latent, preferred_element_type=jnp.float32)
    top_score = jnp.maximum(own_max, new_max)
    old_part = jnp.exp(own_max - top_score)
    new_part = jnp.exp(new_max - top_score)
    numerator = own_acc * old_part[:, None] + new_out * new_part[:, None]
    denominator = own_sum * old_part + new_sum * new_part
    return (numerator / denominator[:, None]).astype(jnp.bfloat16)


def shards(q_latent, q_rope, cache_latent, cache_rope, new_latent, new_rope, removed):
    devices = lax.axis_size("ctx")
    my_index = lax.axis_index("ctx")
    local_blocks, block_rows, lat_width = cache_latent.shape
    head_count, tokens = (q_latent.shape[0], q_latent.shape[1])
    rope_width = new_rope.shape[1]
    own_heads = head_count // devices
    own_count = own_heads * tokens
    total_blocks = local_blocks * devices
    kept_block, drop_before, kept_rows = span_info(removed, total_blocks, block_rows)
    first_block = my_index * local_blocks
    kept_mine = lax.dynamic_slice_in_dim(kept_block, first_block, local_blocks)
    drop_mine = lax.dynamic_slice_in_dim(drop_before, first_block, local_blocks)
    cosine, sine_part = turn_angles(-drop_mine, rope_width)
    cache_keys = rotate_middle(
        cache_rope.astype(jnp.float32), cosine[:, :, None], sine_part[:, :, None]
    ).astype(jnp.bfloat16)
    positions = kept_rows + jnp.arange(tokens, dtype=jnp.int32)
    query_cos, query_sin = turn_angles(positions, rope_width)
    queries_rope = rotate_last(
        q_rope.reshape(head_count, tokens, rope_width).astype(jnp.float32), query_cos, query_sin
    )
    queries_rope = queries_rope.astype(jnp.bfloat16).reshape(head_count * tokens, rope_width)
    new_keys = rotate_last(new_rope.astype(jnp.float32), query_cos, query_sin).astype(jnp.bfloat16)
    query_rows = q_latent.reshape(head_count * tokens, lat_width)
    own_start = my_index * own_count
    own_rows = lax.dynamic_slice_in_dim(query_rows, own_start, own_count, 0)
    own_rope = lax.dynamic_slice_in_dim(queries_rope, own_start, own_count, 0)
    order_slots = jnp.argsort(jnp.logical_not(kept_mine).astype(jnp.int32), stable=True)
    slot_latent = jnp.take(cache_latent, order_slots, axis=0)
    slot_keys = jnp.take(cache_keys, order_slots, axis=0)
    filled = jnp.sum(kept_mine.astype(jnp.int32))

    def kept_step(index_slot, carried):
        latent_block = lax.dynamic_index_in_dim(slot_latent, index_slot, 0, keepdims=False)
        key_block = lax.dynamic_index_in_dim(slot_keys, index_slot, 0, keepdims=False)
        produced = block_terms(query_rows, queries_rope, latent_block, key_block)
        return absorb(carried, produced, jnp.asarray(True))

    run_max, run_sum, run_acc = lax.fori_loop(
        0, filled, kept_step, empty_state(head_count * tokens, lat_width)
    )
    maxima = run_max.reshape(head_count, tokens)
    top_score = lax.pmax(maxima, "ctx")
    factor = jnp.exp(maxima - top_score)
    own_acc, own_sum = (
        lax.psum_scatter(
            run_acc.reshape(head_count, tokens, lat_width) * factor[:, :, None],
            "ctx",
            scatter_dimension=0,
            tiled=True,
        ),
        lax.psum_scatter(
            run_sum.reshape(head_count, tokens) * factor, "ctx", scatter_dimension=0, tiled=True
        ),
    )
    own_max = lax.dynamic_slice_in_dim(top_score, my_index * own_heads, own_heads, 0)
    attended = finish(own_max, own_sum, own_acc, own_rows, own_rope, new_latent, new_keys, tokens)
    return attended.reshape(own_heads, tokens, lat_width)


def solution(mesh):
    in_specs = (
        P(None, "req", None),
        P(None, "req"),
        P(("req", "ctx"), None, None),
        P(("req", "ctx"), None, None),
        P("req", None),
        P("req", None),
        P("req", None),
    )
    out_specs = P("ctx", "req", None)
    return jax.shard_map(shards, mesh=mesh, in_specs=in_specs, out_specs=out_specs, check_vma=False)
```

profile of v0, /device:TPU:0, one launch (start us, length us, event | category | flops | bytes accessed | tf_op | source)
XLA Modules:
  0.0 217.3 jit_solution(2239655744903763529)
XLA Ops:
  6.6 1.4 subtract_reduce_fusion.1
  8.7 0.8 slice_bitcast_fusion.1
  9.6 0.8 convert_reduce_fusion.2
  10.6 0.7 sort.17
  12.1 0.8 convert_element_type.67
  13.0 1.2 copy.23
  14.3 0.8 fusion.25
  17.5 1.8 concatenate.19
  19.8 1.8 concatenate.18
  22.0 3.5 %broadcast_in_dim.57 = f32[3072,512]{1,0:T(8,128)} broadcast(f32[]{:T(128)} %constant.150.clone.1), dimensions={} | broadcast | bytes 6291460 | tf_op jit(solution)/shard_map/broadcast_in_dim | solution.py:105
  25.5 19.4 %while.14 = (s32[]{:T(128)}, f32[3072]{0:T(1024)S(1)}, f32[3072]{0:T(1024)S(1)}, f32[3072,512]{1,0:T(8,128)}, s32[]{:T(128)}, /*index=5*/bf16[4,128,512]{2,1,0:T...) while((s32[]{:T(128)}, f32[3072]{0:T(1024)S(1)}, ...), condition=%wide.region_8.9_spmd, body=%wide.region_5.8_spmd.sunk | while | flops 863907840 | bytes 75161824 | solution.py:173
  26.2 3.2 %fusion.59 = f32[128,3072]{1,0:T(8,128)S(1)} fusion(bf16[3072,512]{1,0:T(8,128)(2,1)} %get-tuple-element.235, bf16[4,128,512]{2,1,0:T(8,128)(2,1)S(1)} %get-tuple-element.234, s32[]{:T(128)S(6)} %select_n.176), kind=kOutput, calls=%fused_computation.8.clone.1 | convolution fusion | flops 402653184 | bytes 4849668 | tf_op jit(solution)/shard_map/while/body/dot_general | solution.py:76
  30.1 2.1 multiply_add_fusion.8
  32.2 2.6 %copy-done.2 = f32[3072,512]{1,0:T(8,128)} copy-done((f32[3072,512]{1,0:T(8,128)}, f32[3072,512]{1,0:T(8,128)S(1)}, u32[]{:S(2)}) %copy-start.2) | copy-done | bytes 6291480 | tf_op jit(solution)/shard_map/while
  35.6 3.2 %fusion.59 = f32[128,3072]{1,0:T(8,128)S(1)} fusion(bf16[3072,512]{1,0:T(8,128)(2,1)} %get-tuple-element.235, bf16[4,128,512]{2,1,0:T(8,128)(2,1)S(1)} %get-tuple-element.234, s32[]{:T(128)S(6)} %select_n.176), kind=kOutput, calls=%fused_computation.8.clone.1 | convolution fusion | flops 402653184 | bytes 4849668 | tf_op jit(solution)/shard_map/while/body/dot_general | solution.py:76
  39.4 2.1 multiply_add_fusion.8
  41.5 2.6 %copy-done.2 = f32[3072,512]{1,0:T(8,128)} copy-done((f32[3072,512]{1,0:T(8,128)}, f32[3072,512]{1,0:T(8,128)S(1)}, u32[]{:S(2)}) %copy-start.2) | copy-done | bytes 6291480 | tf_op jit(solution)/shard_map/while
  45.0 67.4 %pmax.7 = f32[128,24]{1,0:T(8,128)S(1)} all-reduce(f32[128,24]{1,0:T(8,128)S(1)} %reshape.496), channel_id=1, replica_groups=mesh['req'=2,'ctx'=16] {'ctx'}, use_global_device_ids=true, to_apply=%region_9.10 | all-reduce | flops 3072 | bytes 24576 | tf_op jit(solution)/shard_map/pmax | solution.py:177
  112.5 6.0 %broadcast_multiply_fusion = f32[128,24,512]{2,1,0:T(8,128)} fusion(f32[128,24,512]{2,1,0:T(8,128)} %bitcast.44, f32[128,24]{1,0:T(8,128)S(1)} %get-tuple-element.113), kind=kLoop, calls=%fused_computation.20 | loop fusion | flops 1572864 | bytes 12595200 | tf_op jit(solution)/shard_map/mul | solution.py:181
  120.3 58.4 %all-reduce = f32[128,24]{1,0:T(8,128)S(1)} all-reduce(f32[128,24]{1,0:T(8,128)S(1)} %get-tuple-element.112), channel_id=3, replica_groups=mesh['req'=2,'ctx'=16] {'ctx'}, use_global_device_ids=true, to_apply=%region_12.13.clone | all-reduce | flops 3072 | bytes 24576
  178.8 1.1 fusion.16
  180.2 28.2 %reduce-scatter.2.cloned.1.call-done = f32[8,24,512]{2,1,0:T(8,128)} async-done(((f32[128,24,512]{2,1,0:T(8,128)}), f32[8,24,512]{2,1,0:T(8,128)}) %reduce-scatter.2.cloned.1.call-update) | async-done | bytes 393232 | tf_op jit(solution)/shard_map/reduce_scatter | solution.py:180
  208.5 1.1 bitcast_multiply_fusion
  209.6 0.9 fusion.13
  (70 shorter events, 7.6 us)
Async XLA Ops:
  6.5 9.2 %copy-start = (bf16[4,128,512]{2,1,0:T(8,128)(2,1)S(1)}, bf16[4,128,512]{2,1,0:T(8,128)(2,1)}, u32[]{:S(2)}) copy-start(bf16[4,128,512]{2,1,0:T(8,128)(2,1)} %param.17) | copy-start | bytes 1572868
  6.5 10.0 %copy-start.4 = (f32[32]{0:T(128)S(1)}, f32[32]{0:T(128)}, u32[]{:S(2)}) copy-start(f32[32]{0:T(128)} %constant.175.clone) | copy-start | bytes 388
  6.5 10.0 %copy-start.5 = (f32[32]{0:T(128)S(1)}, f32[32]{0:T(128)}, u32[]{:S(2)}) copy-start(f32[32]{0:T(128)} %constant.174.clone) | copy-start | bytes 388
  6.5 10.0 %copy-start.6 = (f32[32]{0:T(128)S(1)}, f32[32]{0:T(128)}, u32[]{:S(2)}) copy-start(f32[32]{0:T(128)} %constant.173.clone) | copy-start | bytes 388
  6.5 201.9 %reduce-scatter.2.cloned.1.call-start = ((), (), s32[]{:S(2)}) async-start(), calls=%async_computation.1 | async-start | bytes 6684672 | tf_op jit(solution)/shard_map/reduce_scatter | solution.py:180
  26.2 3.9 %copy-start.1 = (f32[3072,512]{1,0:T(8,128)S(1)}, f32[3072,512]{1,0:T(8,128)}, u32[]{:S(2)}) copy-start(f32[3072,512]{1,0:T(8,128)} %get-tuple-element.220) | copy-start | bytes 18874372 | tf_op jit(solution)/shard_map/while
  32.2 2.7 %copy-start.2 = (f32[3072,512]{1,0:T(8,128)}, f32[3072,512]{1,0:T(8,128)S(1)}, u32[]{:S(2)}) copy-start(f32[3072,512]{1,0:T(8,128)S(1)} %multiply_add_fusion.8) | copy-start | bytes 18874372 | tf_op jit(solution)/shard_map/while
  35.5 3.9 %copy-start.1 = (f32[3072,512]{1,0:T(8,128)S(1)}, f32[3072,512]{1,0:T(8,128)}, u32[]{:S(2)}) copy-start(f32[3072,512]{1,0:T(8,128)} %get-tuple-element.220) | copy-start | bytes 18874372 | tf_op jit(solution)/shard_map/while
  41.5 2.7 %copy-start.2 = (f32[3072,512]{1,0:T(8,128)}, f32[3072,512]{1,0:T(8,128)S(1)}, u32[]{:S(2)}) copy-start(f32[3072,512]{1,0:T(8,128)S(1)} %multiply_add_fusion.8) | copy-start | bytes 18874372 | tf_op jit(solution)/shard_map/while
  118.5 0.7 copy-start.7
  118.5 60.4 %copy-start.3 = (bf16[24,512]{1,0:T(8,128)(2,1)S(1)}, bf16[24,512]{1,0:T(8,128)(2,1)}, u32[]{:S(2)}) copy-start(bf16[24,512]{1,0:T(8,128)(2,1)} %param.19) | copy-start | bytes 73732
Sparse Core Ops, SparseCore 0:
  118.6 89.8 reduce-scatter.1
where the time goes:
time: 220 us; the launch traced here: 217 us
  blocking collectives  126 us (57%)
  waiting for transfers between devices  28.3 us (13%)
  local copies, waits for them, and re-layouts  18.3 us (8%)
  between operations  15 us (7%)
  other arithmetic  14.1 us (6%)
  matrix products  13.6 us (6%)
  loops' own time  2.23 us (1%)
    pmax x1, blocking collectives, shards(): top_score = lax.pmax(maxima, 'ctx')  67.4 us
    unnamed x1, blocking collectives  58.4 us
    reduce_scatter x1, waiting for transfers between devices, shards(): lax.psum_scatter(run_acc.reshape(head_count, tokens, lat_width) * factor[...  28.2 us
    dot_general x2, matrix products, block_terms(): lax.dot_general(query_rows, latent_block, contract, preferred_element_typ...  6.37 us
    mul x1, other arithmetic, shards(): run_acc.reshape(head_count, tokens, lat_width) * factor[:, :, None]  5.96 us
    while x8, local copies, waits for them, and re-layouts  5.3 us
  transfers between devices with their start and end apart: 1, of which 1 were waited for; matrix products, arithmetic and copies ran while one was open for 1% of the time, Pallas kernels for 0%

commit v1 on v0

v1 whole, which is shorter than its diff:
```python
import jax
import jax.numpy as jnp
import numpy as np
from jax import lax
from jax.experimental import pallas as pl
from jax.experimental.pallas import tpu as pltpu
from jax.sharding import PartitionSpec as P

floor_value = -1e30
score_scale = 192.0 ** (-0.5)


def rope_tables(rope_width):
    halves = rope_width // 2
    frequencies = 10000.0 ** (-2.0 * np.arange(halves) / rope_width)
    coarse = np.mod(4096.0 * frequencies, 2.0 * np.pi)
    middle = np.mod(64.0 * frequencies, 2.0 * np.pi)
    return (
        jnp.asarray(frequencies, jnp.float32),
        jnp.asarray(coarse, jnp.float32),
        jnp.asarray(middle, jnp.float32),
    )


def turn_angles(shift_rows, rope_width):
    frequencies, coarse, middle = rope_tables(rope_width)
    magnitude = jnp.abs(shift_rows)
    signed = jnp.where(shift_rows < 0, -1.0, 1.0).astype(jnp.float32)
    upper_part = (magnitude // 4096).astype(jnp.float32)[..., None]
    centre_part = (magnitude // 64 % 64).astype(jnp.float32)[..., None]
    lowest_part = (magnitude % 64).astype(jnp.float32)[..., None]
    angles = upper_part * coarse + centre_part * middle + lowest_part * frequencies
    return (jnp.cos(angles), signed[..., None] * jnp.sin(angles))


def rotate_last(values, cosine, sine_part):
    halves = values.shape[-1] // 2
    first_half = values[..., :halves]
    second_half = values[..., halves:]
    return jnp.concatenate(
        [
            first_half * cosine - second_half * sine_part,
            first_half * sine_part + second_half * cosine,
        ],
        axis=-1,
    )


def rotate_middle(values, cosine, sine_part):
    halves = values.shape[1] // 2
    first_half = values[:, :halves, :]
    second_half = values[:, halves:, :]
    return jnp.concatenate(
        [
            first_half * cosine - second_half * sine_part,
            first_half * sine_part + second_half * cosine,
        ],
        axis=1,
    )


def span_info(removed, total_blocks, block_rows):
    starts = removed[:, 0]
    finishes = removed[:, 1]
    block_ids = jnp.arange(total_blocks, dtype=jnp.int32)
    inside = (block_ids[:, None] >= starts[None, :]) & (block_ids[:, None] < finishes[None, :])
    kept_block = jnp.logical_not(jnp.any(inside, axis=1))
    drop_before = block_rows * jnp.sum(
        jnp.clip(block_ids[:, None], starts[None, :], finishes[None, :]) - starts[None, :], axis=1
    )
    kept_rows = total_blocks * block_rows - block_rows * jnp.sum(finishes - starts)
    return (kept_block, drop_before, kept_rows)


code_limit = 32767.0
tiny_peak = 1e-30
nt_dims = (((1,), (1,)), ((), ()))


def local_state(q, qr, lat_ref, keys, flag_ref):
    blocks, block_rows, lat_width = lat_ref.shape
    latents = lat_ref[...].reshape(blocks * block_rows, lat_width)
    scores = (
        lax.dot_general(q, latents, nt_dims, preferred_element_type=jnp.float32)
        + jnp.dot(qr, keys, preferred_element_type=jnp.float32)
    ) * score_scale
    lifted, sums, outs = [], [], []
    for b in range(blocks):
        part = scores[:, b * block_rows : (b + 1) * block_rows]
        block_max = jnp.max(part, axis=1, keepdims=True)
        weights = jnp.exp(part - block_max).astype(jnp.bfloat16)
        sums.append(jnp.sum(weights.astype(jnp.float32), axis=1, keepdims=True))
        outs.append(jnp.dot(weights, lat_ref[b], preferred_element_type=jnp.float32))
        lifted.append(jnp.where(flag_ref[b] > 0, block_max, floor_value))
    top = lifted[0]
    for b in range(1, blocks):
        top = jnp.maximum(top, lifted[b])
    total, acc = 0.0, 0.0
    for b in range(blocks):
        factor = jnp.where(flag_ref[b] > 0, jnp.exp(lifted[b] - top), 0.0)
        total = total + sums[b] * factor
        acc = acc + outs[b] * factor
    return top, total, acc


def merge(one, other):
    top = jnp.maximum(one[0], other[0])
    left, right = jnp.exp(one[0] - top), jnp.exp(other[0] - top)
    return top, one[1] * left + other[1] * right, one[2] * left + other[2] * right


def put_state(state, code_ref, meta_ref, slot):
    top, total, acc = state
    rows = acc.shape[0]
    peak = jnp.maximum(jnp.max(jnp.abs(acc), axis=1, keepdims=True), tiny_peak)
    code_ref[slot] = jnp.round(acc * (code_limit / peak)).astype(jnp.int32).astype(jnp.int16)
    lane = lax.broadcasted_iota(jnp.int32, (rows, 128), 1)
    packed = jnp.where(lane == 0, top, jnp.where(lane == 1, total, peak * (1.0 / code_limit)))
    spare = meta_ref.shape[2] - rows
    if spare:
        packed = jnp.concatenate([packed, jnp.zeros((spare, 128), jnp.float32)], axis=0)
    meta_ref[slot] = packed.T[:8]


def get_state(code_ref, meta_ref, slot):
    rows = code_ref.shape[1]
    meta = meta_ref[slot]
    meta = jnp.concatenate([meta, jnp.zeros((120, meta.shape[1]), jnp.float32)], axis=0).T[:rows]
    acc = code_ref[slot].astype(jnp.int32).astype(jnp.float32) * meta[:, 2:3]
    return meta[:, 0:1], meta[:, 1:2], acc


def new_state(q, qr, lat, keys, tokens):
    rows = q.shape[0]
    scores = (
        lax.dot_general(q, lat, nt_dims, preferred_element_type=jnp.float32)
        + lax.dot_general(qr, keys, nt_dims, preferred_element_type=jnp.float32)
    ) * score_scale
    token = lax.broadcasted_iota(jnp.int32, (rows, tokens), 0) % tokens
    causal = lax.broadcasted_iota(jnp.int32, (rows, tokens), 1) <= token
    masked = jnp.where(causal, scores, floor_value)
    top = jnp.max(masked, axis=1, keepdims=True)
    weights = jnp.where(causal, jnp.exp(masked - top), 0.0).astype(jnp.bfloat16)
    total = jnp.sum(weights.astype(jnp.float32), axis=1, keepdims=True)
    return top, total, jnp.dot(weights, lat, preferred_element_type=jnp.float32)


def exchange_kernel(
    far, tokens, q_ref, qr_ref, lat_ref, key_ref, flag_ref, new_lat_ref, new_key_ref, out_ref,
    core_out, core_in, core_out_meta, core_in_meta,
    pair_out, pair_in, pair_out_meta, pair_in_meta,
    far_out, far_in, far_out_meta, far_in_meta,
    core_sems, pair_sems, far_sems,
):
    me = lax.axis_index("ctx")
    core, pair, place = me % 2, (me // 2) % 2, me // 4

    def index_of(place_id, pair_id, core_id):
        return (place_id * 2 + pair_id) * 2 + core_id

    def place_at(step):
        return (place + 1 + step) % far

    sibling = index_of(place, pair, 1 - core)
    partner = index_of(place, 1 - pair, core)
    barrier = pltpu.get_barrier_semaphore()
    for other in [sibling, partner]:
        pl.semaphore_signal(barrier, 1, device_id={"ctx": other})

    def greet(step, nothing):
        pl.semaphore_signal(barrier, 1, device_id={"ctx": index_of(place_at(step), pair, core)})
        return nothing

    lax.fori_loop(0, far - 1, greet, 0)
    pl.semaphore_wait(barrier, far + 1)

    def copies(source, landing, source_meta, landing_meta, sems, slot, target):
        return [
            pltpu.make_async_remote_copy(
                src_ref=a.at[slot],
                dst_ref=b.at[slot],
                send_sem=sems.at[2 * kind, slot],
                recv_sem=sems.at[2 * kind + 1, slot],
                device_id={"ctx": target},
            )
            for kind, (a, b) in enumerate([(source, landing), (source_meta, landing_meta)])
        ]

    def core_copies(slot):
        return copies(core_out, core_in, core_out_meta, core_in_meta, core_sems, slot, sibling)

    def pair_copies(slot):
        return copies(pair_out, pair_in, pair_out_meta, pair_in_meta, pair_sems, slot, partner)

    def far_copies(slot):
        target = index_of(place_at(slot), pair, core)
        return copies(far_out, far_in, far_out_meta, far_in_meta, far_sems, slot, target)

    def start(both):
        for copy in both:
            copy.start()

    def landed(both):
        for copy in both:
            copy.wait_recv()

    def own_state(owner):
        return local_state(q_ref[owner], qr_ref[owner], lat_ref, key_ref[...], flag_ref)

    def to_core(pair_id, first):
        def step_of(step, nothing):
            state = own_state(index_of(place_at(step), pair_id, 1 - core))
            put_state(state, core_out, core_out_meta, first + step)
            start(core_copies(first + step))
            return nothing

        lax.fori_loop(0, far, step_of, 0)

    to_core(1 - pair, 0)

    def to_pair(step, nothing):
        state = own_state(index_of(place_at(step), 1 - pair, core))
        landed(core_copies(step))
        state = merge(state, get_state(core_in, core_in_meta, step))
        put_state(state, pair_out, pair_out_meta, step)
        start(pair_copies(step))
        return nothing

    lax.fori_loop(0, far, to_pair, 0)
    to_core(pair, far)

    def gathered(step):
        state = own_state(index_of(place_at(step), pair, core))
        landed(core_copies(far + step))
        state = merge(state, get_state(core_in, core_in_meta, far + step))
        landed(pair_copies(step))
        return merge(state, get_state(pair_in, pair_in_meta, step))

    def to_far(step, nothing):
        put_state(gathered(step), far_out, far_out_meta, step)
        start(far_copies(step))
        return nothing

    lax.fori_loop(0, far - 1, to_far, 0)
    state = gathered(far - 1)
    state = merge(
        state, new_state(q_ref[me], qr_ref[me], new_lat_ref[...], new_key_ref[...], tokens)
    )

    def take_far(step, carried):
        landed(far_copies(step))
        return merge(carried, get_state(far_in, far_in_meta, step))

    top, total, acc = lax.fori_loop(0, far - 1, take_far, state)
    out_ref[...] = (acc / total).astype(out_ref.dtype)

    def sent(make, count):
        def step_of(step, nothing):
            for copy in make(step):
                copy.wait_send()
            return nothing

        lax.fori_loop(0, count, step_of, 0)

    sent(core_copies, 2 * far)
    sent(pair_copies, far)
    sent(far_copies, far - 1)


def shards(q_latent, q_rope, cache_latent, cache_rope, new_latent, new_rope, removed):
    devices = lax.axis_size("ctx")
    my_index = lax.axis_index("ctx")
    local_blocks, block_rows, lat_width = cache_latent.shape
    head_count, tokens = (q_latent.shape[0], q_latent.shape[1])
    rope_width = new_rope.shape[1]
    own_heads = head_count // devices
    own_count = own_heads * tokens
    total_blocks = local_blocks * devices
    far = devices // 4
    kept_block, drop_before, kept_rows = span_info(removed, total_blocks, block_rows)
    first_block = my_index * local_blocks
    kept_mine = lax.dynamic_slice_in_dim(kept_block, first_block, local_blocks)
    drop_mine = lax.dynamic_slice_in_dim(drop_before, first_block, local_blocks)
    cosine, sine_part = turn_angles(-drop_mine, rope_width)
    cache_keys = rotate_middle(
        cache_rope.astype(jnp.float32), cosine[:, :, None], sine_part[:, :, None]
    ).astype(jnp.bfloat16)
    key_columns = jnp.transpose(cache_keys, (1, 0, 2)).reshape(rope_width, local_blocks * block_rows)
    positions = kept_rows + jnp.arange(tokens, dtype=jnp.int32)
    query_cos, query_sin = turn_angles(positions, rope_width)
    queries_rope = rotate_last(
        q_rope.reshape(head_count, tokens, rope_width).astype(jnp.float32), query_cos, query_sin
    )
    queries_rope = queries_rope.astype(jnp.bfloat16).reshape(devices, own_count, rope_width)
    new_keys = rotate_last(new_rope.astype(jnp.float32), query_cos, query_sin).astype(jnp.bfloat16)
    query_rows = q_latent.reshape(devices, own_count, lat_width)
    meta_rows = -(-own_count // 128) * 128

    def room(slots):
        return [pltpu.VMEM((slots, own_count, lat_width), jnp.int16)] * 2 + [
            pltpu.VMEM((slots, 8, meta_rows), jnp.float32)
        ] * 2

    vmem = pl.BlockSpec(memory_space=pltpu.VMEM)
    rows = head_count * tokens
    keys = local_blocks * block_rows
    attended = pl.pallas_call(
        lambda *refs: exchange_kernel(far, tokens, *refs),
        out_shape=jax.ShapeDtypeStruct((own_count, lat_width), jnp.bfloat16),
        in_specs=[vmem] * 4 + [pl.BlockSpec(memory_space=pltpu.SMEM)] + [vmem] * 2,
        out_specs=vmem,
        scratch_shapes=room(2 * far) + room(far) + room(far - 1) + [
            pltpu.SemaphoreType.DMA((4, 2 * far)),
            pltpu.SemaphoreType.DMA((4, far)),
            pltpu.SemaphoreType.DMA((4, far - 1)),
        ],
        compiler_params=pltpu.CompilerParams(
            collective_id=0, has_side_effects=True, vmem_limit_bytes=48 * 1024 * 1024
        ),
        cost_estimate=pl.CostEstimate(
            flops=2 * rows * keys * (2 * lat_width + rope_width),
            bytes_accessed=2 * (rows + keys) * (lat_width + rope_width),
            transcendentals=rows * keys,
        ),
    )(
        query_rows, queries_rope, cache_latent, key_columns, kept_mine.astype(jnp.int32),
        new_latent, new_keys,
    )
    return attended.reshape(own_heads, tokens, lat_width)


def solution(mesh):
    in_specs = (
        P(None, "req", None),
        P(None, "req"),
        P(("req", "ctx"), None, None),
        P(("req", "ctx"), None, None),
        P("req", None),
        P("req", None),
        P("req", None),
    )
    out_specs = P("ctx", "req", None)
    return jax.shard_map(shards, mesh=mesh, in_specs=in_specs, out_specs=out_specs, check_vma=False)
```

time: 220 us -> 47 us (0.21)
  the two profiles are of different devices: /device:TPU:0 before, /device:TPU:9 now
where the time goes in v1:
time: 47 us; the launch traced here: 46.8 us
  Pallas kernels  38.9 us (83%)
  local copies, waits for them, and re-layouts  4.72 us (10%)
  other arithmetic  2.31 us (5%)
  between operations  0.88 us (2%)
    pallas_call x1, Pallas kernels, shards(): pl.pallas_call(lambda *refs: exchange_kernel(far, tokens, *refs), out_sha...  38.9 us
    unnamed x20, local copies, waits for them, and re-layouts  3.87 us

profile of v1, /device:TPU:9, one launch (start us, length us, event | category | flops | bytes accessed | tf_op | source)
XLA Modules:
  0.0 46.8 jit_solution(16129651500450734112)
XLA Ops:
  0.0 0.0 copy-start.4
  0.0 0.0 copy-start.8
  0.0 1.3 %copy.19 = bf16[128,1536]{0,1:T(8,128)(2,1)S(1)} copy(bf16[128,1536]{1,0:T(8,128)(2,1)} %param.14) | data formatting | bytes 786432 | tf_op args[1]
  1.3 0.1 convert.27
  1.4 0.0 copy-done.4
  1.4 0.6 %subtract_reduce_fusion.1 = s32[]{:T(128)} fusion(s32[12,2]{0,1:T(2,128)S(1)} %copy-done.8), kind=kLoop, calls=%fused_computation.55 | loop fusion | flops 23 | bytes 100 | tf_op jit(solution)/shard_map/reduce_sum | solution.py:71
  2.8 0.1 subtract_convert_fusion.2
  2.9 0.3 subtract_convert_fusion
  3.2 0.4 copy.21
  3.6 0.0 copy-start.3
  3.6 0.4 copy.20
  4.1 0.0 copy-start.1
  4.1 0.0 copy-start.2
  4.1 0.4 pad_maximum_fusion.refs_1_
  4.6 0.1 subtract_reduce_fusion
  4.7 0.1 fusion.12
  4.8 0.1 fusion.3
  4.9 0.1 subtract_convert_fusion.1
  5.1 0.1 fusion.2
  5.2 0.1 dynamic-slice_convert_fusion.refs_4_
  5.2 0.1 pad_maximum_fusion.1.refs_6_
  5.3 1.9 %copy-done = bf16[128,24,512]{2,1,0:T(8,128)(2,1)S(1)} copy-done((bf16[128,24,512]{2,1,0:T(8,128)(2,1)S(1)}, bf16[128,24,512]{2,1,0:T(8,128)(2,1)}, u32[]{:S(2)}) %copy-start) | copy-done | bytes 3145752
  7.2 38.9 %shard_map.127 = bf16[192,512]{1,0:T(8,128)(2,1)S(1)} custom-call(bf16[16,192,512]{2,1,0:T(8,128)(2,1)S(1)} %bitcast.21, bf16[16,192,64]{2,1,0:T(8,128)(2,1)S(1)} %pad_maximum_fusion.refs_1_, bf16[4,128,512]{2,1,0:T(8,128)(2,1)S(1)} %copy-done.1, bf16[64,512]{1,0:T(8,128)(2,1)S(1)} %copy_bitcast_fusion.refs_3_, s32[4]{0:T(128)S(1)} %dynamic-slice_convert_fusion.refs_4_, ...), custom_call_target="tpu_custom_call" | custom-call | flops 3422552064 | bytes 4128768 | tf_op jit(solution)/shard_map/pallas_call | solution.py:307
  46.1 0.7 %copy.26 = bf16[8,24,512]{2,1,0:T(8,128)(2,1)} copy(bf16[8,24,512]{2,1,0:T(8,128)(2,1)S(1)} %bitcast.20) | data formatting | bytes 393216
  (23 shorter events, 0.1 us)
Async XLA Ops:
  0.0 2.8 %copy-start.5 = (f32[32]{0:T(128)S(1)}, f32[32]{0:T(128)}, u32[]{:S(2)}) copy-start(f32[32]{0:T(128)} %constant.99.clone) | copy-start | bytes 388
  0.0 2.8 %copy-start.6 = (f32[32]{0:T(128)S(1)}, f32[32]{0:T(128)}, u32[]{:S(2)}) copy-start(f32[32]{0:T(128)} %constant.101.clone) | copy-start | bytes 388
  0.0 2.8 %copy-start.7 = (f32[32]{0:T(128)S(1)}, f32[32]{0:T(128)}, u32[]{:S(2)}) copy-start(f32[32]{0:T(128)} %constant.100.clone) | copy-start | bytes 388
  0.0 1.4 %copy-start.4 = (bf16[24,64]{1,0:T(8,128)(2,1)S(1)}, bf16[24,64]{1,0:T(8,128)(2,1)}, u32[]{:S(2)}) copy-start(bf16[24,64]{1,0:T(8,128)(2,1)} %param.18) | copy-start | bytes 9220
  0.0 1.4 %copy-start.8 = (s32[12,2]{0,1:T(2,128)S(1)}, s32[12,2]{0,1:T(2,128)}, u32[]{:S(2)}) copy-start(s32[12,2]{0,1:T(2,128)} %param.19) | copy-start | bytes 292
  3.6 0.9 %copy-start.3 = (bf16[4,64,128]{2,1,0:T(8,128)(2,1)S(1)}, bf16[4,64,128]{2,1,0:T(8,128)(2,1)}, u32[]{:S(2)}) copy-start(bf16[4,64,128]{2,1,0:T(8,128)(2,1)} %param.16) | copy-start | bytes 196612
  4.1 1.2 %copy-start.1 = (bf16[4,128,512]{2,1,0:T(8,128)(2,1)S(1)}, bf16[4,128,512]{2,1,0:T(8,128)(2,1)}, u32[]{:S(2)}) copy-start(bf16[4,128,512]{2,1,0:T(8,128)(2,1)} %refs_2_.1) | copy-start | bytes 1572868
  4.1 1.2 %copy-start.2 = (bf16[24,512]{1,0:T(8,128)(2,1)S(1)}, bf16[24,512]{1,0:T(8,128)(2,1)}, u32[]{:S(2)}) copy-start(bf16[24,512]{1,0:T(8,128)(2,1)} %refs_5_.1) | copy-start | bytes 73732
  5.3 1.9 %copy-start = (bf16[128,24,512]{2,1,0:T(8,128)(2,1)S(1)}, bf16[128,24,512]{2,1,0:T(8,128)(2,1)}, u32[]{:S(2)}) copy-start(bf16[128,24,512]{2,1,0:T(8,128)(2,1)} %param.13) | copy-start | bytes 9437188

commit v2 on v1

--- a/solution.py
+++ b/solution.py
@@ -145,13 +145,19 @@
     return top, total, jnp.dot(weights, lat, preferred_element_type=jnp.float32)
 
 
+def half_of(state, second, rows):
+    return tuple(jnp.where(second, part[rows:], part[:rows]) for part in state)
+
+
 def exchange_kernel(
     far, tokens, q_ref, qr_ref, lat_ref, key_ref, flag_ref, new_lat_ref, new_key_ref, out_ref,
     core_out, core_in, core_out_meta, core_in_meta,
     pair_out, pair_in, pair_out_meta, pair_in_meta,
     far_out, far_in, far_out_meta, far_in_meta,
-    core_sems, pair_sems, far_sems,
+    q_buf, held_acc, held_rows,
+    core_sems, pair_sems, far_sems, q_sems,
 ):
+    own = out_ref.shape[0]
     me = lax.axis_index("ctx")
     core, pair, place = me % 2, (me // 2) % 2, me // 4
 
@@ -161,6 +167,18 @@
     def place_at(step):
         return (place + 1 + step) % far
 
+    def chip_at(step):
+        pair_id = (pair + 1 + step // far) % 2
+        return place_at(step % far) * 2 + pair_id
+
+    def q_copy(step):
+        return pltpu.make_async_copy(q_ref.at[chip_at(step)], q_buf.at[step], q_sems.at[step])
+
+    def fetch(step, nothing):
+        q_copy(step).start()
+        return nothing
+
+    lax.fori_loop(0, 2 * far, fetch, 0)
     sibling = index_of(place, pair, 1 - core)
     partner = index_of(place, 1 - pair, core)
     barrier = pltpu.get_barrier_semaphore()
@@ -204,35 +222,39 @@
         for copy in both:
             copy.wait_recv()
 
-    def own_state(owner):
-        return local_state(q_ref[owner], qr_ref[owner], lat_ref, key_ref[...], flag_ref)
-
-    def to_core(pair_id, first):
-        def step_of(step, nothing):
-            state = own_state(index_of(place_at(step), pair_id, 1 - core))
-            put_state(state, core_out, core_out_meta, first + step)
-            start(core_copies(first + step))
-            return nothing
-
-        lax.fori_loop(0, far, step_of, 0)
-
-    to_core(1 - pair, 0)
-
-    def to_pair(step, nothing):
-        state = own_state(index_of(place_at(step), 1 - pair, core))
-        landed(core_copies(step))
-        state = merge(state, get_state(core_in, core_in_meta, step))
-        put_state(state, pair_out, pair_out_meta, step)
-        start(pair_copies(step))
+    def hold(state, slot):
+        top, total, acc = state
+        lane = lax.broadcasted_iota(jnp.int32, (own, 128), 1)
+        held_rows[slot] = jnp.where(lane == 0, top, total)
+        held_acc[slot] = acc
+
+    def with_sibling(slot):
+        rows = held_rows[slot]
+        state = rows[:, 0:1], rows[:, 1:2], held_acc[slot]
+        landed(core_copies(slot))
+        return merge(state, get_state(core_in, core_in_meta, slot))
+
+    def chip_step(step, nothing):
+        q_copy(step).wait()
+        states = local_state(q_buf[step], qr_ref[chip_at(step)], lat_ref, key_ref[...], flag_ref)
+        put_state(half_of(states, core == 0, own), core_out, core_out_meta, step)
+        start(core_copies(step))
+        hold(half_of(states, core == 1, own), step)
+
+        @pl.when((step >= 1) & (step <= far))
+        def to_pair():
+            put_state(with_sibling(step - 1), pair_out, pair_out_meta, step - 1)
+            start(pair_copies(step - 1))
+
         return nothing
 
-    lax.fori_loop(0, far, to_pair, 0)
-    to_core(pair, far)
+    lax.fori_loop(0, 2 * far, chip_step, 0)
+    last = 2 * far - 1
+    fresh = new_state(q_buf[last], qr_ref[chip_at(last)], new_lat_ref[...], new_key_ref[...], tokens)
+    fresh = half_of(fresh, core == 1, own)
 
     def gathered(step):
-        state = own_state(index_of(place_at(step), pair, core))
-        landed(core_copies(far + step))
-        state = merge(state, get_state(core_in, core_in_meta, far + step))
+        state = with_sibling(far + step)
         landed(pair_copies(step))
         return merge(state, get_state(pair_in, pair_in_meta, step))
 
@@ -242,10 +264,7 @@
         return nothing
 
     lax.fori_loop(0, far - 1, to_far, 0)
-    state = gathered(far - 1)
-    state = merge(
-        state, new_state(q_ref[me], qr_ref[me], new_lat_ref[...], new_key_ref[...], tokens)
-    )
+    state = merge(gathered(far - 1), fresh)
 
     def take_far(step, carried):
         landed(far_copies(step))
@@ -291,9 +310,9 @@
     queries_rope = rotate_last(
         q_rope.reshape(head_count, tokens, rope_width).astype(jnp.float32), query_cos, query_sin
     )
-    queries_rope = queries_rope.astype(jnp.bfloat16).reshape(devices, own_count, rope_width)
+    queries_rope = queries_rope.astype(jnp.bfloat16).reshape(devices // 2, 2 * own_count, rope_width)
     new_keys = rotate_last(new_rope.astype(jnp.float32), query_cos, query_sin).astype(jnp.bfloat16)
-    query_rows = q_latent.reshape(devices, own_count, lat_width)
+    query_rows = q_latent.reshape(devices // 2, 2 * own_count, lat_width)
     meta_rows = -(-own_count // 128) * 128
 
     def room(slots):
@@ -307,12 +326,16 @@
     attended = pl.pallas_call(
         lambda *refs: exchange_kernel(far, tokens, *refs),
         out_shape=jax.ShapeDtypeStruct((own_count, lat_width), jnp.bfloat16),
-        in_specs=[vmem] * 4 + [pl.BlockSpec(memory_space=pltpu.SMEM)] + [vmem] * 2,
+        in_specs=[pl.BlockSpec(memory_space=pl.ANY)] + [vmem] * 3 + [pl.BlockSpec(memory_space=pltpu.SMEM)] + [vmem] * 2,
         out_specs=vmem,
         scratch_shapes=room(2 * far) + room(far) + room(far - 1) + [
+            pltpu.VMEM((2 * far, 2 * own_count, lat_width), jnp.bfloat16),
+            pltpu.VMEM((2 * far, own_count, lat_width), jnp.float32),
+            pltpu.VMEM((2 * far, own_count, 128), jnp.float32),
             pltpu.SemaphoreType.DMA((4, 2 * far)),
             pltpu.SemaphoreType.DMA((4, far)),
             pltpu.SemaphoreType.DMA((4, far - 1)),
+            pltpu.SemaphoreType.DMA((2 * far,)),
         ],
         compiler_params=pltpu.CompilerParams(
             collective_id=0, has_side_effects=True, vmem_limit_bytes=48 * 1024 * 1024

time: 47 us -> 49.6 us (1.055)
  Pallas kernels: 38.9 us -> 41.5 us
    pallas_call x1, Pallas kernels: 38.9 us -> 41.5 us  [shards(): pl.pallas_call(lambda *refs: exchange_kernel(far, tokens, *refs), out_sha...]
where the time goes in v2:
time: 49.6 us; the launch traced here: 49.4 us
  Pallas kernels  41.5 us (84%)
  local copies, waits for them, and re-layouts  4.72 us (10%)
  other arithmetic  2.3 us (5%)
  between operations  0.88 us (2%)
    pallas_call x1, Pallas kernels, shards(): pl.pallas_call(lambda *refs: exchange_kernel(far, tokens, *refs), out_sha...  41.5 us
    unnamed x20, local copies, waits for them, and re-layouts  3.87 us

profile of v2, /device:TPU:9, one launch (start us, length us, event | category | flops | bytes accessed | tf_op | source)
XLA Modules:
  0.0 49.4 jit_solution(9112795591217866427)
XLA Ops:
  0.0 0.0 copy-start.4
  0.0 0.0 copy-start.8
  0.0 1.3 %copy.19 = bf16[128,1536]{0,1:T(8,128)(2,1)S(1)} copy(bf16[128,1536]{1,0:T(8,128)(2,1)} %param.14) | data formatting | bytes 786432 | tf_op args[1]
  1.3 0.1 convert.27
  1.4 0.0 copy-done.4
  1.4 0.6 %subtract_reduce_fusion.1 = s32[]{:T(128)} fusion(s32[12,2]{0,1:T(2,128)S(1)} %copy-done.8), kind=kLoop, calls=%fused_computation.55 | loop fusion | flops 23 | bytes 100 | tf_op jit(solution)/shard_map/reduce_sum | solution.py:71
  2.8 0.1 subtract_convert_fusion.2
  2.9 0.3 subtract_convert_fusion
  3.2 0.4 copy.21
  3.6 0.0 copy-start.3
  3.6 0.4 copy.20
  4.1 0.0 copy-start.1
  4.1 0.0 copy-start.2
  4.1 0.4 pad_maximum_fusion.refs_1_
  4.6 0.1 subtract_reduce_fusion
  4.7 0.1 fusion.12
  4.8 0.1 fusion.3
  4.9 0.1 subtract_convert_fusion.1
  5.1 0.1 fusion.2
  5.2 0.1 dynamic-slice_convert_fusion.refs_4_
  5.2 0.1 pad_maximum_fusion.1.refs_6_
  5.3 1.9 %copy-done = bf16[128,24,512]{2,1,0:T(8,128)(2,1)S(1)} copy-done((bf16[128,24,512]{2,1,0:T(8,128)(2,1)S(1)}, bf16[128,24,512]{2,1,0:T(8,128)(2,1)}, u32[]{:S(2)}) %copy-start) | copy-done | bytes 3145752
  7.2 41.5 %shard_map.127 = bf16[192,512]{1,0:T(8,128)(2,1)S(1)} custom-call(bf16[8,384,512]{2,1,0:T(8,128)(2,1)S(1)} %bitcast.21, bf16[8,384,64]{2,1,0:T(8,128)(2,1)S(1)} %pad_maximum_fusion.refs_1_, bf16[4,128,512]{2,1,0:T(8,128)(2,1)S(1)} %copy-done.1, bf16[64,512]{1,0:T(8,128)(2,1)S(1)} %copy_bitcast_fusion.refs_3_, s32[4]{0:T(128)S(1)} %dynamic-slice_convert_fusion.refs_4_, ...), custom_call_target="tpu_custom_call" | custom-call | flops 3422552064 | bytes 4128768 | tf_op jit(solution)/shard_map/pallas_call | solution.py:326
  48.7 0.7 %copy.26 = bf16[8,24,512]{2,1,0:T(8,128)(2,1)} copy(bf16[8,24,512]{2,1,0:T(8,128)(2,1)S(1)} %bitcast.20) | data formatting | bytes 393216
  (23 shorter events, 0.1 us)
Async XLA Ops:
  0.0 2.8 %copy-start.5 = (f32[32]{0:T(128)S(1)}, f32[32]{0:T(128)}, u32[]{:S(2)}) copy-start(f32[32]{0:T(128)} %constant.99.clone) | copy-start | bytes 388
  0.0 2.8 %copy-start.6 = (f32[32]{0:T(128)S(1)}, f32[32]{0:T(128)}, u32[]{:S(2)}) copy-start(f32[32]{0:T(128)} %constant.101.clone) | copy-start | bytes 388
  0.0 2.8 %copy-start.7 = (f32[32]{0:T(128)S(1)}, f32[32]{0:T(128)}, u32[]{:S(2)}) copy-start(f32[32]{0:T(128)} %constant.100.clone) | copy-start | bytes 388
  0.0 1.4 %copy-start.4 = (bf16[24,64]{1,0:T(8,128)(2,1)S(1)}, bf16[24,64]{1,0:T(8,128)(2,1)}, u32[]{:S(2)}) copy-start(bf16[24,64]{1,0:T(8,128)(2,1)} %param.18) | copy-start | bytes 9220
  0.0 1.4 %copy-start.8 = (s32[12,2]{0,1:T(2,128)S(1)}, s32[12,2]{0,1:T(2,128)}, u32[]{:S(2)}) copy-start(s32[12,2]{0,1:T(2,128)} %param.19) | copy-start | bytes 292
  3.6 0.9 %copy-start.3 = (bf16[4,64,128]{2,1,0:T(8,128)(2,1)S(1)}, bf16[4,64,128]{2,1,0:T(8,128)(2,1)}, u32[]{:S(2)}) copy-start(bf16[4,64,128]{2,1,0:T(8,128)(2,1)} %param.16) | copy-start | bytes 196612
  4.1 1.2 %copy-start.1 = (bf16[4,128,512]{2,1,0:T(8,128)(2,1)S(1)}, bf16[4,128,512]{2,1,0:T(8,128)(2,1)}, u32[]{:S(2)}) copy-start(bf16[4,128,512]{2,1,0:T(8,128)(2,1)} %refs_2_.1) | copy-start | bytes 1572868
  4.1 1.2 %copy-start.2 = (bf16[24,512]{1,0:T(8,128)(2,1)S(1)}, bf16[24,512]{1,0:T(8,128)(2,1)}, u32[]{:S(2)}) copy-start(bf16[24,512]{1,0:T(8,128)(2,1)} %refs_5_.1) | copy-start | bytes 73732
  5.3 1.9 %copy-start = (bf16[128,24,512]{2,1,0:T(8,128)(2,1)S(1)}, bf16[128,24,512]{2,1,0:T(8,128)(2,1)}, u32[]{:S(2)}) copy-start(bf16[128,24,512]{2,1,0:T(8,128)(2,1)} %param.13) | copy-start | bytes 9437188

commit v3 on v2

--- a/solution.py
+++ b/solution.py
@@ -75,32 +75,42 @@
 code_limit = 32767.0
 tiny_peak = 1e-30
 nt_dims = (((1,), (1,)), ((), ()))
-
-
-def local_state(q, qr, lat_ref, keys, flag_ref):
+tn_dims = (((0,), (0,)), ((), ()))
+
+
+def block_weights(q, qr, lat_ref, keys, flag_ref):
     blocks, block_rows, lat_width = lat_ref.shape
     latents = lat_ref[...].reshape(blocks * block_rows, lat_width)
     scores = (
-        lax.dot_general(q, latents, nt_dims, preferred_element_type=jnp.float32)
-        + jnp.dot(qr, keys, preferred_element_type=jnp.float32)
+        lax.dot_general(latents, q, nt_dims, preferred_element_type=jnp.float32)
+        + lax.dot_general(keys, qr, nt_dims, preferred_element_type=jnp.float32)
     ) * score_scale
-    lifted, sums, outs = [], [], []
+    lifted, sums, weights = [], [], []
     for b in range(blocks):
-        part = scores[:, b * block_rows : (b + 1) * block_rows]
-        block_max = jnp.max(part, axis=1, keepdims=True)
-        weights = jnp.exp(part - block_max).astype(jnp.bfloat16)
-        sums.append(jnp.sum(weights.astype(jnp.float32), axis=1, keepdims=True))
-        outs.append(jnp.dot(weights, lat_ref[b], preferred_element_type=jnp.float32))
+        part = scores[b * block_rows : (b + 1) * block_rows]
+        block_max = jnp.max(part, axis=0, keepdims=True)
+        weights.append(jnp.exp(part - block_max).astype(jnp.bfloat16))
+        sums.append(jnp.sum(weights[b].astype(jnp.float32), axis=0, keepdims=True))
         lifted.append(jnp.where(flag_ref[b] > 0, block_max, floor_value))
     top = lifted[0]
     for b in range(1, blocks):
         top = jnp.maximum(top, lifted[b])
-    total, acc = 0.0, 0.0
-    for b in range(blocks):
-        factor = jnp.where(flag_ref[b] > 0, jnp.exp(lifted[b] - top), 0.0)
-        total = total + sums[b] * factor
-        acc = acc + outs[b] * factor
-    return top, total, acc
+    factors = [jnp.where(flag_ref[b] > 0, jnp.exp(lifted[b] - top), 0.0) for b in range(blocks)]
+    total = sum(sums[b] * factors[b] for b in range(blocks))
+    return top, total, weights, factors
+
+
+def weighted(columns, weights, factors):
+    block_rows = weights[0].shape[0]
+    return sum(
+        jnp.dot(
+            columns[:, b * block_rows : (b + 1) * block_rows],
+            weights[b],
+            preferred_element_type=jnp.float32,
+        )
+        * factors[b]
+        for b in range(len(weights))
+    )
 
 
 def merge(one, other):
@@ -111,53 +121,43 @@
 
 def put_state(state, code_ref, meta_ref, slot):
     top, total, acc = state
-    rows = acc.shape[0]
-    peak = jnp.maximum(jnp.max(jnp.abs(acc), axis=1, keepdims=True), tiny_peak)
+    peak = jnp.maximum(jnp.max(jnp.abs(acc), axis=0, keepdims=True), tiny_peak)
     code_ref[slot] = jnp.round(acc * (code_limit / peak)).astype(jnp.int32).astype(jnp.int16)
-    lane = lax.broadcasted_iota(jnp.int32, (rows, 128), 1)
-    packed = jnp.where(lane == 0, top, jnp.where(lane == 1, total, peak * (1.0 / code_limit)))
-    spare = meta_ref.shape[2] - rows
-    if spare:
-        packed = jnp.concatenate([packed, jnp.zeros((spare, 128), jnp.float32)], axis=0)
-    meta_ref[slot] = packed.T[:8]
+    meta_ref[slot, 0:1] = top
+    meta_ref[slot, 1:2] = total
+    meta_ref[slot, 2:3] = peak * (1.0 / code_limit)
 
 
 def get_state(code_ref, meta_ref, slot):
-    rows = code_ref.shape[1]
-    meta = meta_ref[slot]
-    meta = jnp.concatenate([meta, jnp.zeros((120, meta.shape[1]), jnp.float32)], axis=0).T[:rows]
-    acc = code_ref[slot].astype(jnp.int32).astype(jnp.float32) * meta[:, 2:3]
-    return meta[:, 0:1], meta[:, 1:2], acc
-
-
-def new_state(q, qr, lat, keys, tokens):
-    rows = q.shape[0]
+    acc = code_ref[slot].astype(jnp.int32).astype(jnp.float32) * meta_ref[slot, 2:3]
+    return meta_ref[slot, 0:1], meta_ref[slot, 1:2], acc
+
+
+def new_state(q, qr, lat, half, keys):
+    tokens, rows = lat.shape[0], q.shape[0]
     scores = (
-        lax.dot_general(q, lat, nt_dims, preferred_element_type=jnp.float32)
-        + lax.dot_general(qr, keys, nt_dims, preferred_element_type=jnp.float32)
+        lax.dot_general(lat, q, nt_dims, preferred_element_type=jnp.float32)
+        + lax.dot_general(keys, qr, nt_dims, preferred_element_type=jnp.float32)
     ) * score_scale
-    token = lax.broadcasted_iota(jnp.int32, (rows, tokens), 0) % tokens
-    causal = lax.broadcasted_iota(jnp.int32, (rows, tokens), 1) <= token
+    token = lax.broadcasted_iota(jnp.int32, (tokens, rows), 1) % tokens
+    causal = lax.broadcasted_iota(jnp.int32, (tokens, rows), 0) <= token
     masked = jnp.where(causal, scores, floor_value)
-    top = jnp.max(masked, axis=1, keepdims=True)
+    top = jnp.max(masked, axis=0, keepdims=True)
     weights = jnp.where(causal, jnp.exp(masked - top), 0.0).astype(jnp.bfloat16)
-    total = jnp.sum(weights.astype(jnp.float32), axis=1, keepdims=True)
-    return top, total, jnp.dot(weights, lat, preferred_element_type=jnp.float32)
-
-
-def half_of(state, second, rows):
-    return tuple(jnp.where(second, part[rows:], part[:rows]) for part in state)
+    total = jnp.sum(weights.astype(jnp.float32), axis=0, keepdims=True)
+    return top, total, lax.dot_general(half, weights, tn_dims, preferred_element_type=jnp.float32)
 
 
 def exchange_kernel(
-    far, tokens, q_ref, qr_ref, lat_ref, key_ref, flag_ref, new_lat_ref, new_key_ref, out_ref,
+    far, q_ref, qr_ref, lat_ref, key_ref, flag_ref, new_lat_ref, new_key_ref, out_ref,
     core_out, core_in, core_out_meta, core_in_meta,
     pair_out, pair_in, pair_out_meta, pair_in_meta,
     far_out, far_in, far_out_meta, far_in_meta,
-    q_buf, held_acc, held_rows,
-    core_sems, pair_sems, far_sems, q_sems,
+    q_buf, columns, held_acc, held_rows, swap_out, swap_in,
+    core_sems, pair_sems, far_sems, q_sems, swap_sems,
 ):
-    own = out_ref.shape[0]
+    own, lat_width = out_ref.shape
+    width = lat_width // 2
     me = lax.axis_index("ctx")
     core, pair, place = me % 2, (me // 2) % 2, me // 4
 
@@ -190,6 +190,9 @@
         return nothing
 
     lax.fori_loop(0, far - 1, greet, 0)
+    turned = lat_ref[...].reshape(columns.shape[2], lat_width).T
+    columns[0] = turned[:width]
+    columns[1] = turned[width:]
     pl.semaphore_wait(barrier, far + 1)
 
     def copies(source, landing, source_meta, landing_meta, sems, slot, target):
@@ -222,48 +225,44 @@
         for copy in both:
             copy.wait_recv()
 
-    def hold(state, slot):
-        top, total, acc = state
-        lane = lax.broadcasted_iota(jnp.int32, (own, 128), 1)
-        held_rows[slot] = jnp.where(lane == 0, top, total)
-        held_acc[slot] = acc
-
     def with_sibling(slot):
-        rows = held_rows[slot]
-        state = rows[:, 0:1], rows[:, 1:2], held_acc[slot]
+        state = held_rows[slot, 0:1], held_rows[slot, 1:2], held_acc[slot]
         landed(core_copies(slot))
         return merge(state, get_state(core_in, core_in_meta, slot))
 
+    def gathered(step):
+        state = with_sibling(far + step)
+        landed(pair_copies(step))
+        return merge(state, get_state(pair_in, pair_in_meta, step))
+
     def chip_step(step, nothing):
         q_copy(step).wait()
-        states = local_state(q_buf[step], qr_ref[chip_at(step)], lat_ref, key_ref[...], flag_ref)
-        put_state(half_of(states, core == 0, own), core_out, core_out_meta, step)
+        top, total, weights, factors = block_weights(
+            q_buf[step], qr_ref[chip_at(step)], lat_ref, key_ref[...], flag_ref
+        )
+        theirs = weighted(columns[1 - core], weights, factors)
+        put_state((top, total, theirs), core_out, core_out_meta, step)
         start(core_copies(step))
-        hold(half_of(states, core == 1, own), step)
+        held_rows[step, 0:1] = top
+        held_rows[step, 1:2] = total
+        held_acc[step] = weighted(columns[core], weights, factors)
 
         @pl.when((step >= 1) & (step <= far))
         def to_pair():
             put_state(with_sibling(step - 1), pair_out, pair_out_meta, step - 1)
             start(pair_copies(step - 1))
 
+        @pl.when(step > far)
+        def to_far():
+            put_state(gathered(step - 1 - far), far_out, far_out_meta, step - 1 - far)
+            start(far_copies(step - 1 - far))
+
         return nothing
 
     lax.fori_loop(0, 2 * far, chip_step, 0)
     last = 2 * far - 1
-    fresh = new_state(q_buf[last], qr_ref[chip_at(last)], new_lat_ref[...], new_key_ref[...], tokens)
-    fresh = half_of(fresh, core == 1, own)
-
-    def gathered(step):
-        state = with_sibling(far + step)
-        landed(pair_copies(step))
-        return merge(state, get_state(pair_in, pair_in_meta, step))
-
-    def to_far(step, nothing):
-        put_state(gathered(step), far_out, far_out_meta, step)
-        start(far_copies(step))
-        return nothing
-
-    lax.fori_loop(0, far - 1, to_far, 0)
+    half = jnp.where(core == 0, new_lat_ref[:, :width], new_lat_ref[:, width:])
+    fresh = new_state(q_buf[last], qr_ref[chip_at(last)], new_lat_ref[...], half, new_key_ref[...])
     state = merge(gathered(far - 1), fresh)
 
     def take_far(step, carried):
@@ -271,7 +270,22 @@
         return merge(carried, get_state(far_in, far_in_meta, step))
 
     top, total, acc = lax.fori_loop(0, far - 1, take_far, state)
-    out_ref[...] = (acc / total).astype(out_ref.dtype)
+    done = acc / total
+    spare = -done.shape[1] % 128
+    if spare:
+        done = jnp.concatenate([done, jnp.zeros((width, spare), jnp.float32)], axis=1)
+    done = done.T
+    first, second = done[:own], done[own : 2 * own]
+    swap_out[...] = jnp.where(core == 0, second, first).astype(out_ref.dtype)
+    swap = pltpu.make_async_remote_copy(
+        src_ref=swap_out,
+        dst_ref=swap_in,
+        send_sem=swap_sems.at[0],
+        recv_sem=swap_sems.at[1],
+        device_id={"ctx": sibling},
+    )
+    swap.start()
+    kept = jnp.where(core == 0, first, second)
 
     def sent(make, count):
         def step_of(step, nothing):
@@ -284,6 +298,10 @@
     sent(core_copies, 2 * far)
     sent(pair_copies, far)
     sent(far_copies, far - 1)
+    swap.wait()
+    other = swap_in[...].astype(jnp.float32)
+    out_ref[:, :width] = jnp.where(core == 0, kept, other).astype(out_ref.dtype)
+    out_ref[:, width:] = jnp.where(core == 0, other, kept).astype(out_ref.dtype)
 
 
 def shards(q_latent, q_rope, cache_latent, cache_rope, new_latent, new_rope, removed):
@@ -304,7 +322,7 @@
     cache_keys = rotate_middle(
         cache_rope.astype(jnp.float32), cosine[:, :, None], sine_part[:, :, None]
     ).astype(jnp.bfloat16)
-    key_columns = jnp.transpose(cache_keys, (1, 0, 2)).reshape(rope_width, local_blocks * block_rows)
+    key_rows = jnp.transpose(cache_keys, (0, 2, 1)).reshape(local_blocks * block_rows, rope_width)
     positions = kept_rows + jnp.arange(tokens, dtype=jnp.int32)
     query_cos, query_sin = turn_angles(positions, rope_width)
     queries_rope = rotate_last(
@@ -313,32 +331,37 @@
     queries_rope = queries_rope.astype(jnp.bfloat16).reshape(devices // 2, 2 * own_count, rope_width)
     new_keys = rotate_last(new_rope.astype(jnp.float32), query_cos, query_sin).astype(jnp.bfloat16)
     query_rows = q_latent.reshape(devices // 2, 2 * own_count, lat_width)
-    meta_rows = -(-own_count // 128) * 128
+    chip_rows = 2 * own_count
+    width = lat_width // 2
 
     def room(slots):
-        return [pltpu.VMEM((slots, own_count, lat_width), jnp.int16)] * 2 + [
-            pltpu.VMEM((slots, 8, meta_rows), jnp.float32)
+        return [pltpu.VMEM((slots, width, chip_rows), jnp.int16)] * 2 + [
+            pltpu.VMEM((slots, 8, chip_rows), jnp.float32)
         ] * 2
 
     vmem = pl.BlockSpec(memory_space=pltpu.VMEM)
     rows = head_count * tokens
     keys = local_blocks * block_rows
     attended = pl.pallas_call(
-        lambda *refs: exchange_kernel(far, tokens, *refs),
+        lambda *refs: exchange_kernel(far, *refs),
         out_shape=jax.ShapeDtypeStruct((own_count, lat_width), jnp.bfloat16),
         in_specs=[pl.BlockSpec(memory_space=pl.ANY)] + [vmem] * 3 + [pl.BlockSpec(memory_space=pltpu.SMEM)] + [vmem] * 2,
         out_specs=vmem,
         scratch_shapes=room(2 * far) + room(far) + room(far - 1) + [
-            pltpu.VMEM((2 * far, 2 * own_count, lat_width), jnp.bfloat16),
-            pltpu.VMEM((2 * far, own_count, lat_width), jnp.float32),
-            pltpu.VMEM((2 * far, own_count, 128), jnp.float32),
+            pltpu.VMEM((2 * far, chip_rows, lat_width), jnp.bfloat16),
+            pltpu.VMEM((2, width, keys), jnp.bfloat16),
+            pltpu.VMEM((2 * far, width, chip_rows), jnp.float32),
+            pltpu.VMEM((2 * far, 8, chip_rows), jnp.float32),
+            pltpu.VMEM((own_count, width), jnp.bfloat16),
+            pltpu.VMEM((own_count, width), jnp.bfloat16),
             pltpu.SemaphoreType.DMA((4, 2 * far)),
             pltpu.SemaphoreType.DMA((4, far)),
             pltpu.SemaphoreType.DMA((4, far - 1)),
             pltpu.SemaphoreType.DMA((2 * far,)),
+            pltpu.SemaphoreType.DMA((2,)),
         ],
         compiler_params=pltpu.CompilerParams(
-            collective_id=0, has_side_effects=True, vmem_limit_bytes=48 * 1024 * 1024
+            collective_id=0, has_side_effects=True, vmem_limit_bytes=60 * 1024 * 1024
         ),
         cost_estimate=pl.CostEstimate(
             flops=2 * rows * keys * (2 * lat_width + rope_width),
@@ -346,7 +369,7 @@
             transcendentals=rows * keys,
         ),
     )(
-        query_rows, queries_rope, cache_latent, key_columns, kept_mine.astype(jnp.int32),
+        query_rows, queries_rope, cache_latent, key_rows, kept_mine.astype(jnp.int32),
         new_latent, new_keys,
     )
     return attended.reshape(own_heads, tokens, lat_width)

time: 49.6 us -> 47 us (0.948)
  the two profiles are of different devices: /device:TPU:9 before, /device:TPU:0 now
where the time goes in v3:
time: 47 us; the launch traced here: 46.9 us
  Pallas kernels  37.1 us (79%)
  local copies, waits for them, and re-layouts  4.54 us (10%)
  other arithmetic  4.36 us (9%)
  between operations  0.83 us (2%)
    pallas_call x1, Pallas kernels, shards(): pl.pallas_call(lambda *refs: exchange_kernel(far, *refs), out_shape=jax.S...  37.1 us
    unnamed x14, local copies, waits for them, and re-layouts  2.92 us
    concatenate x2, other arithmetic, rotate_last(): jnp.concatenate([first_half * cosine - second_half * sine_part, first_hal...  1.99 us

profile of v3, /device:TPU:0, one launch (start us, length us, event | category | flops | bytes accessed | tf_op | source)
XLA Modules:
  0.0 46.9 jit_solution(800634817897387277)
XLA Ops:
  0.0 1.3 %copy.19 = bf16[128,1536]{0,1:T(8,128)(2,1)S(1)} copy(bf16[128,1536]{1,0:T(8,128)(2,1)} %param.14) | data formatting | bytes 786432 | tf_op args[1]
  1.3 0.1 convert.27
  1.4 0.0 copy-done.1
  1.4 0.0 copy-done.5
  1.4 0.6 %subtract_reduce_fusion.1 = s32[]{:T(128)} fusion(s32[12,2]{0,1:T(2,128)S(1)} %copy-done.5), kind=kLoop, calls=%fused_computation.54 | loop fusion | flops 23 | bytes 100 | tf_op jit(solution)/shard_map/reduce_sum | solution.py:71
  2.8 0.0 copy-done.2
  2.8 0.0 copy-done.3
  2.8 0.0 copy-done.4
  2.8 0.1 subtract_convert_fusion.2
  2.9 0.3 subtract_convert_fusion
  3.2 0.4 copy.21
  3.6 0.0 copy-start
  3.6 0.4 copy.20
  4.1 1.3 %pad_maximum_fusion.refs_1_ = bf16[8,384,64]{2,1,0:T(8,128)(2,1)} fusion(bf16[8,384,32]{2,1,0:T(8,128)(2,1)S(1)} %bitcast.17, bf16[8,384,32]{2,1,0:T(8,128)(2,1)S(1)} %bitcast.18), kind=kLoop, calls=%fused_computation | loop fusion | flops 786432 | bytes 786432 | tf_op jit(solution)/shard_map/concatenate | solution.py:40
  5.4 0.1 subtract_reduce_fusion
  5.5 0.1 fusion.12
  5.7 0.1 fusion.3
  5.8 0.1 subtract_convert_fusion.1
  5.9 0.8 %copy.22 = bf16[4,128,64]{2,1,0:T(8,128)(2,1)} copy(bf16[4,128,64]{1,2,0:T(8,128)(2,1)S(1)} %maximum_bitcast_fusion) | data formatting | bytes 131072 | tf_op jit(solution)/shard_map/transpose | solution.py:325
  6.7 0.1 fusion.2
  6.8 0.6 %dynamic-slice_convert_fusion.refs_4_ = s32[4]{0:T(128)} fusion(pred[64]{0:T(512)(128)(4,1)S(1)} %not.3, s32[]{:T(128)S(6)} %select_n.74), kind=kLoop, calls=%fused_computation.23 | loop fusion | flops 4 | bytes 24 | tf_op jit(solution)/shard_map/convert_element_type | solution.py:372
  7.4 0.7 %pad_maximum_fusion.1.refs_6_ = bf16[24,64]{1,0:T(8,128)(2,1)} fusion(bf16[24,32]{1,0:T(8,128)(2,1)S(1)} %get-tuple-element.14, bf16[24,32]{1,0:T(8,128)(2,1)S(1)} %get-tuple-element.13), kind=kLoop, calls=%fused_computation.16 | loop fusion | flops 6144 | bytes 6144 | tf_op jit(solution)/shard_map/concatenate | solution.py:40
  8.1 37.1 %shard_map.127 = bf16[192,512]{1,0:T(8,128)(2,1)} custom-call(bf16[8,384,512]{2,1,0:T(8,128)(2,1)} %bitcast.22, bf16[8,384,64]{2,1,0:T(8,128)(2,1)} %pad_maximum_fusion.refs_1_, bf16[4,128,512]{2,1,0:T(8,128)(2,1)} %refs_2_.1, bf16[512,64]{1,0:T(8,128)(2,1)} %bitcast.21, s32[4]{0:T(128)} %dynamic-slice_convert_fusion.refs_4_, bf16[24,512]{1,0:T(8,128)(2,1)} %refs_5_.1, ...), custom_call_target="tpu_custom_call" | custom-call | flops 3422552064 | bytes 4128768 | tf_op jit(solution)/shard_map/pallas_call | solution.py:345
  45.2 1.6 %copy.24 = bf16[8,24,512]{2,1,0:T(8,128)(2,1)} copy(bf16[8,24,512]{2,1,0:T(8,128)(2,1)} %bitcast.20) | data formatting | bytes 393216
  (18 shorter events, 0.1 us)
Async XLA Ops:
  0.0 2.8 %copy-start.2 = (f32[32]{0:T(128)S(1)}, f32[32]{0:T(128)}, u32[]{:S(2)}) copy-start(f32[32]{0:T(128)} %constant.99.clone) | copy-start | bytes 388
  0.0 2.8 %copy-start.3 = (f32[32]{0:T(128)S(1)}, f32[32]{0:T(128)}, u32[]{:S(2)}) copy-start(f32[32]{0:T(128)} %constant.101.clone) | copy-start | bytes 388
  0.0 2.8 %copy-start.4 = (f32[32]{0:T(128)S(1)}, f32[32]{0:T(128)}, u32[]{:S(2)}) copy-start(f32[32]{0:T(128)} %constant.100.clone) | copy-start | bytes 388
  0.0 1.4 %copy-start.1 = (bf16[24,64]{1,0:T(8,128)(2,1)S(1)}, bf16[24,64]{1,0:T(8,128)(2,1)}, u32[]{:S(2)}) copy-start(bf16[24,64]{1,0:T(8,128)(2,1)} %param.18) | copy-start | bytes 9220
  0.0 1.4 %copy-start.5 = (s32[12,2]{0,1:T(2,128)S(1)}, s32[12,2]{0,1:T(2,128)}, u32[]{:S(2)}) copy-start(s32[12,2]{0,1:T(2,128)} %param.19) | copy-start | bytes 292
  3.6 1.8 %copy-start = (bf16[4,64,128]{2,1,0:T(8,128)(2,1)S(1)}, bf16[4,64,128]{2,1,0:T(8,128)(2,1)}, u32[]{:S(2)}) copy-start(bf16[4,64,128]{2,1,0:T(8,128)(2,1)} %param.16) | copy-start | bytes 196612

commit v4 on v3

--- a/solution.py
+++ b/solution.py
@@ -15,61 +15,41 @@
     frequencies = 10000.0 ** (-2.0 * np.arange(halves) / rope_width)
     coarse = np.mod(4096.0 * frequencies, 2.0 * np.pi)
     middle = np.mod(64.0 * frequencies, 2.0 * np.pi)
-    return (
-        jnp.asarray(frequencies, jnp.float32),
-        jnp.asarray(coarse, jnp.float32),
-        jnp.asarray(middle, jnp.float32),
-    )
-
-
-def turn_angles(shift_rows, rope_width):
-    frequencies, coarse, middle = rope_tables(rope_width)
-    magnitude = jnp.abs(shift_rows)
-    signed = jnp.where(shift_rows < 0, -1.0, 1.0).astype(jnp.float32)
-    upper_part = (magnitude // 4096).astype(jnp.float32)[..., None]
-    centre_part = (magnitude // 64 % 64).astype(jnp.float32)[..., None]
-    lowest_part = (magnitude % 64).astype(jnp.float32)[..., None]
-    angles = upper_part * coarse + centre_part * middle + lowest_part * frequencies
-    return (jnp.cos(angles), signed[..., None] * jnp.sin(angles))
-
-
-def rotate_last(values, cosine, sine_part):
-    halves = values.shape[-1] // 2
-    first_half = values[..., :halves]
-    second_half = values[..., halves:]
-    return jnp.concatenate(
-        [
-            first_half * cosine - second_half * sine_part,
-            first_half * sine_part + second_half * cosine,
-        ],
-        axis=-1,
-    )
-
-
-def rotate_middle(values, cosine, sine_part):
-    halves = values.shape[1] // 2
-    first_half = values[:, :halves, :]
-    second_half = values[:, halves:, :]
-    return jnp.concatenate(
-        [
-            first_half * cosine - second_half * sine_part,
-            first_half * sine_part + second_half * cosine,
-        ],
-        axis=1,
-    )
-
-
-def span_info(removed, total_blocks, block_rows):
-    starts = removed[:, 0]
-    finishes = removed[:, 1]
-    block_ids = jnp.arange(total_blocks, dtype=jnp.int32)
-    inside = (block_ids[:, None] >= starts[None, :]) & (block_ids[:, None] < finishes[None, :])
-    kept_block = jnp.logical_not(jnp.any(inside, axis=1))
-    drop_before = block_rows * jnp.sum(
-        jnp.clip(block_ids[:, None], starts[None, :], finishes[None, :]) - starts[None, :], axis=1
-    )
-    kept_rows = total_blocks * block_rows - block_rows * jnp.sum(finishes - starts)
-    return (kept_block, drop_before, kept_rows)
+    tables = np.zeros((halves + 8, 128), np.float32)
+    for digit, table in enumerate([coarse, middle, frequencies]):
+        tables[:halves, digit] = table
+        tables[halves + digit] = np.tile(table, 128 // halves)
+    return tables
+
+
+def angles_of(rows, coarse, middle, lowest):
+    upper_part = (rows >> 12).astype(jnp.float32)
+    centre_part = ((rows >> 6) & 63).astype(jnp.float32)
+    lowest_part = (rows & 63).astype(jnp.float32)
+    return upper_part * coarse + centre_part * middle + lowest_part * lowest
+
+
+def span_scalars(removed_ref, first_block, local_blocks, total_blocks, block_rows):
+    inside = [0] * local_blocks
+    drops = [0] * local_blocks
+    gone = 0
+    for span in range(removed_ref.shape[0]):
+        first, last = removed_ref[span, 0], removed_ref[span, 1]
+        gone = gone + (last - first)
+        for b in range(local_blocks):
+            block = first_block + b
+            inside[b] = inside[b] + jnp.where((block >= first) & (block < last), 1, 0)
+            drops[b] = drops[b] + jnp.minimum(jnp.maximum(block, first), last) - first
+    return inside, [block_rows * drop for drop in drops], block_rows * (total_blocks - gone)
+
+
+def turn_slab(slab, cosine, signed_sine, rope_width):
+    halves = rope_width // 2
+    lane = lax.broadcasted_iota(jnp.int32, slab.shape, 1)
+    swapped = jnp.where(
+        lane % rope_width < halves, pltpu.roll(slab, 128 - halves, 1), pltpu.roll(slab, halves, 1)
+    )
+    return slab * cosine + swapped * signed_sine
 
 
 code_limit = 32767.0
@@ -78,7 +58,7 @@
 tn_dims = (((0,), (0,)), ((), ()))
 
 
-def block_weights(q, qr, lat_ref, keys, flag_ref):
+def block_weights(q, qr, lat_ref, keys, inside):
     blocks, block_rows, lat_width = lat_ref.shape
     latents = lat_ref[...].reshape(blocks * block_rows, lat_width)
     scores = (
@@ -91,11 +71,11 @@
         block_max = jnp.max(part, axis=0, keepdims=True)
         weights.append(jnp.exp(part - block_max).astype(jnp.bfloat16))
         sums.append(jnp.sum(weights[b].astype(jnp.float32), axis=0, keepdims=True))
-        lifted.append(jnp.where(flag_ref[b] > 0, block_max, floor_value))
+        lifted.append(jnp.where(inside[b] == 0, block_max, floor_value))
     top = lifted[0]
     for b in range(1, blocks):
         top = jnp.maximum(top, lifted[b])
-    factors = [jnp.where(flag_ref[b] > 0, jnp.exp(lifted[b] - top), 0.0) for b in range(blocks)]
+    factors = [jnp.where(inside[b] == 0, jnp.exp(lifted[b] - top), 0.0) for b in range(blocks)]
     total = sum(sums[b] * factors[b] for b in range(blocks))
     return top, total, weights, factors
 
@@ -149,11 +129,12 @@
 
 
 def exchange_kernel(
-    far, q_ref, qr_ref, lat_ref, key_ref, flag_ref, new_lat_ref, new_key_ref, out_ref,
+    far, q_ref, rope_ref, lat_ref, cache_rope_ref, new_lat_ref, new_rope_ref, removed_ref, table_ref, out_ref,
     core_out, core_in, core_out_meta, core_in_meta,
     pair_out, pair_in, pair_out_meta, pair_in_meta,
     far_out, far_in, far_out_meta, far_in_meta,
     q_buf, columns, held_acc, held_rows, swap_out, swap_in,
+    key_rows, new_keys, slab_cos, slab_sin, pick,
     core_sems, pair_sems, far_sems, q_sems, swap_sems,
 ):
     own, lat_width = out_ref.shape
@@ -190,9 +171,73 @@
         return nothing
 
     lax.fori_loop(0, far - 1, greet, 0)
+    blocks, block_rows = lat_ref.shape[:2]
+    tokens, rope_width = new_rope_ref.shape
+    halves, group = rope_width // 2, 128 // rope_width
+    slabs = tokens // group
     turned = lat_ref[...].reshape(columns.shape[2], lat_width).T
     columns[0] = turned[:width]
     columns[1] = turned[width:]
+    inside, drops, kept_rows = span_scalars(
+        removed_ref, me * blocks, blocks, blocks * 4 * far, block_rows
+    )
+    along = [table_ref[halves + digit : halves + digit + 1] for digit in range(3)]
+    down = [table_ref[:halves, digit : digit + 1] for digit in range(3)]
+
+    def signed(sine):
+        lane = lax.broadcasted_iota(jnp.int32, sine.shape, 1)
+        return jnp.where(lane % rope_width < halves, -sine, sine)
+
+    row = lax.broadcasted_iota(jnp.int32, (slabs, 128), 0)
+    lane = lax.broadcasted_iota(jnp.int32, (slabs, 128), 1)
+    angles = angles_of(kept_rows + row * group + lane // rope_width, *along)
+    slab_cos[...] = jnp.cos(angles)
+    slab_sin[...] = signed(jnp.sin(angles))
+    angles = angles_of(kept_rows + lax.broadcasted_iota(jnp.int32, (tokens, 128), 0), *along)
+    fresh_rope = jnp.concatenate([new_rope_ref[...].astype(jnp.float32)] * group, axis=1)
+    new_keys[...] = turn_slab(
+        fresh_rope, jnp.cos(angles), signed(jnp.sin(angles)), rope_width
+    ).astype(jnp.bfloat16)
+    lane = lax.broadcasted_iota(jnp.int32, (halves, 128), 1)
+    dropped = jnp.zeros((halves, 128), jnp.int32)
+    for b in range(blocks):
+        dropped = jnp.where(lane == b, drops[b], dropped)
+    angles = angles_of(dropped, *down)
+    cosine, sine = jnp.cos(angles), -jnp.sin(angles)
+    for b in range(blocks):
+        c, s = cosine[:, b : b + 1], sine[:, b : b + 1]
+        first = cache_rope_ref[b, :halves].astype(jnp.float32)
+        second = cache_rope_ref[b, halves:].astype(jnp.float32)
+        keys = jnp.concatenate([first * c - second * s, first * s + second * c] * group, axis=0)
+        key_rows[b * block_rows : (b + 1) * block_rows] = keys.T.astype(jnp.bfloat16)
+    heads = rope_ref.shape[1]
+    head_rows = pick.shape[1] // slabs
+    row = lax.broadcasted_iota(jnp.int32, pick.shape, 0)
+    column = lax.broadcasted_iota(jnp.int32, pick.shape, 1)
+    chosen = (row % tokens) // group * head_rows + row // tokens
+    pick[...] = jnp.where(column == chosen, 1.0, 0.0).astype(jnp.bfloat16)
+
+    def rope_rows(chip):
+        values = rope_ref[chip].astype(jnp.float32)
+        if head_rows > heads:
+            spare = jnp.zeros((head_rows - heads, values.shape[1]), jnp.float32)
+            values = jnp.concatenate([values, spare], axis=0)
+        turned = [
+            turn_slab(
+                values[:, j * 128 : (j + 1) * 128],
+                slab_cos[j : j + 1],
+                slab_sin[j : j + 1],
+                rope_width,
+            )
+            for j in range(slabs)
+        ]
+        stacked = jnp.concatenate(turned, axis=0).astype(jnp.bfloat16)
+        rows = jnp.dot(pick[...], stacked, preferred_element_type=jnp.float32)
+        row = lax.broadcasted_iota(jnp.int32, rows.shape, 0)
+        lane = lax.broadcasted_iota(jnp.int32, rows.shape, 1)
+        own_lanes = lane // rope_width == row % tokens % group
+        return jnp.where(own_lanes, rows, 0.0).astype(jnp.bfloat16)
+
     pl.semaphore_wait(barrier, far + 1)
 
     def copies(source, landing, source_meta, landing_meta, sems, slot, target):
@@ -238,7 +283,7 @@
     def chip_step(step, nothing):
         q_copy(step).wait()
         top, total, weights, factors = block_weights(
-            q_buf[step], qr_ref[chip_at(step)], lat_ref, key_ref[...], flag_ref
+            q_buf[step], rope_rows(chip_at(step)), lat_ref, key_rows[...], inside
         )
         theirs = weighted(columns[1 - core], weights, factors)
         put_state((top, total, theirs), core_out, core_out_meta, step)
@@ -262,7 +307,9 @@
     lax.fori_loop(0, 2 * far, chip_step, 0)
     last = 2 * far - 1
     half = jnp.where(core == 0, new_lat_ref[:, :width], new_lat_ref[:, width:])
-    fresh = new_state(q_buf[last], qr_ref[chip_at(last)], new_lat_ref[...], half, new_key_ref[...])
+    fresh = new_state(
+        q_buf[last], rope_rows(chip_at(last)), new_lat_ref[...], half, new_keys[...]
+    )
     state = merge(gathered(far - 1), fresh)
 
     def take_far(step, carried):
@@ -306,33 +353,19 @@
 
 def shards(q_latent, q_rope, cache_latent, cache_rope, new_latent, new_rope, removed):
     devices = lax.axis_size("ctx")
-    my_index = lax.axis_index("ctx")
     local_blocks, block_rows, lat_width = cache_latent.shape
     head_count, tokens = (q_latent.shape[0], q_latent.shape[1])
     rope_width = new_rope.shape[1]
     own_heads = head_count // devices
     own_count = own_heads * tokens
-    total_blocks = local_blocks * devices
     far = devices // 4
-    kept_block, drop_before, kept_rows = span_info(removed, total_blocks, block_rows)
-    first_block = my_index * local_blocks
-    kept_mine = lax.dynamic_slice_in_dim(kept_block, first_block, local_blocks)
-    drop_mine = lax.dynamic_slice_in_dim(drop_before, first_block, local_blocks)
-    cosine, sine_part = turn_angles(-drop_mine, rope_width)
-    cache_keys = rotate_middle(
-        cache_rope.astype(jnp.float32), cosine[:, :, None], sine_part[:, :, None]
-    ).astype(jnp.bfloat16)
-    key_rows = jnp.transpose(cache_keys, (0, 2, 1)).reshape(local_blocks * block_rows, rope_width)
-    positions = kept_rows + jnp.arange(tokens, dtype=jnp.int32)
-    query_cos, query_sin = turn_angles(positions, rope_width)
-    queries_rope = rotate_last(
-        q_rope.reshape(head_count, tokens, rope_width).astype(jnp.float32), query_cos, query_sin
-    )
-    queries_rope = queries_rope.astype(jnp.bfloat16).reshape(devices // 2, 2 * own_count, rope_width)
-    new_keys = rotate_last(new_rope.astype(jnp.float32), query_cos, query_sin).astype(jnp.bfloat16)
-    query_rows = q_latent.reshape(devices // 2, 2 * own_count, lat_width)
+    chips = devices // 2
     chip_rows = 2 * own_count
     width = lat_width // 2
+    rows = head_count * tokens
+    keys = local_blocks * block_rows
+    slabs = tokens * rope_width // 128
+    head_rows = -(-2 * own_heads // 8) * 8
 
     def room(slots):
         return [pltpu.VMEM((slots, width, chip_rows), jnp.int16)] * 2 + [
@@ -340,12 +373,12 @@
         ] * 2
 
     vmem = pl.BlockSpec(memory_space=pltpu.VMEM)
-    rows = head_count * tokens
-    keys = local_blocks * block_rows
     attended = pl.pallas_call(
         lambda *refs: exchange_kernel(far, *refs),
         out_shape=jax.ShapeDtypeStruct((own_count, lat_width), jnp.bfloat16),
-        in_specs=[pl.BlockSpec(memory_space=pl.ANY)] + [vmem] * 3 + [pl.BlockSpec(memory_space=pltpu.SMEM)] + [vmem] * 2,
+        in_specs=[pl.BlockSpec(memory_space=pl.ANY)]
+        + [vmem] * 5
+        + [pl.BlockSpec(memory_space=pltpu.SMEM), vmem],
         out_specs=vmem,
         scratch_shapes=room(2 * far) + room(far) + room(far - 1) + [
             pltpu.VMEM((2 * far, chip_rows, lat_width), jnp.bfloat16),
@@ -354,6 +387,11 @@
             pltpu.VMEM((2 * far, 8, chip_rows), jnp.float32),
             pltpu.VMEM((own_count, width), jnp.bfloat16),
             pltpu.VMEM((own_count, width), jnp.bfloat16),
+            pltpu.VMEM((keys, 128), jnp.bfloat16),
+            pltpu.VMEM((tokens, 128), jnp.bfloat16),
+            pltpu.VMEM((slabs, 128), jnp.float32),
+            pltpu.VMEM((slabs, 128), jnp.float32),
+            pltpu.VMEM((chip_rows, slabs * head_rows), jnp.bfloat16),
             pltpu.SemaphoreType.DMA((4, 2 * far)),
             pltpu.SemaphoreType.DMA((4, far)),
             pltpu.SemaphoreType.DMA((4, far - 1)),
@@ -369,8 +407,10 @@
             transcendentals=rows * keys,
         ),
     )(
-        query_rows, queries_rope, cache_latent, key_rows, kept_mine.astype(jnp.int32),
-        new_latent, new_keys,
+        q_latent.reshape(chips, chip_rows, lat_width),
+        q_rope.reshape(chips, 2 * own_heads, tokens * rope_width),
+        cache_latent, cache_rope, new_latent, new_rope, removed,
+        jnp.asarray(rope_tables(rope_width)),
     )
     return attended.reshape(own_heads, tokens, lat_width)
 

time: 47 us -> 40.5 us (0.86)
  other arithmetic: 4.36 us -> 0 us
  local copies, waits for them, and re-layouts: 4.54 us -> 2.97 us
  between operations: 0.83 us -> 0.01 us
    concatenate x2 -> x0, other arithmetic: 1.99 us -> none  [rotate_last(): jnp.concatenate([first_half * cosine - second_half * sine_part, first_hal...]
    convert_element_type x9 -> x0, other arithmetic: 0.89 us -> none  [the longest x1 0.65 us: shards(): kept_mine.astype(jnp.int32)]
    another operation x2 -> x0, local copies, waits for them, and re-layouts: 0.85 us -> none
    transpose x1 -> x0, local copies, waits for them, and re-layouts: 0.77 us -> none  [shards(): jnp.transpose(cache_keys, (0, 2, 1))]
    reduce_sum x2 -> x0, other arithmetic: 0.72 us -> none  [the longest x1 0.63 us: span_info(): jnp.sum(finishes - starts)]
    another operation x3 -> x0, other arithmetic: 0.52 us -> none
    unnamed x14 -> x2, local copies, waits for them, and re-layouts: 2.92 us -> 2.97 us
where the time goes in v4:
time: 40.5 us; the launch traced here: 40 us
  Pallas kernels  37 us (91%)
  local copies, waits for them, and re-layouts  2.97 us (7%)
    pallas_call x1, Pallas kernels, shards(): pl.pallas_call(lambda *refs: exchange_kernel(far, *refs), out_shape=jax.S...  37 us
    unnamed x2, local copies, waits for them, and re-layouts  2.97 us

profile of v4, /device:TPU:0, one launch (start us, length us, event | category | flops | bytes accessed | tf_op | source)
XLA Modules:
  0.0 40.0 jit_solution(13570937926994923740)
XLA Ops:
  0.0 1.4 %copy.9.refs_6_ = s32[12,2]{1,0:T(8,128)} copy(s32[12,2]{0,1:T(2,128)} %param.14) | data formatting | bytes 192 | tf_op args[6]
  1.4 37.0 %shard_map.82 = bf16[192,512]{1,0:T(8,128)(2,1)} custom-call(bf16[8,384,512]{2,1,0:T(8,128)(2,1)} %bitcast.4, bf16[8,16,1536]{2,1,0:T(8,128)(2,1)} %bitcast.5, bf16[4,128,512]{2,1,0:T(8,128)(2,1)} %refs_2_.1, bf16[4,64,128]{2,1,0:T(8,128)(2,1)} %refs_3_.1, bf16[24,512]{1,0:T(8,128)(2,1)} %refs_4_.1, bf16[24,64]{1,0:T(8,128)(2,1)} %refs_5_.1, ...), custom_call_target="tpu_custom_call" | custom-call | flops 3422552064 | bytes 4128768 | tf_op jit(solution)/shard_map/pallas_call | solution.py:376
  38.4 1.6 %copy.11 = bf16[8,24,512]{2,1,0:T(8,128)(2,1)} copy(bf16[8,24,512]{2,1,0:T(8,128)(2,1)} %bitcast.3) | data formatting | bytes 393216

commit v5 on v4

--- a/solution.py
+++ b/solution.py
@@ -33,8 +33,8 @@
     inside = [0] * local_blocks
     drops = [0] * local_blocks
     gone = 0
-    for span in range(removed_ref.shape[0]):
-        first, last = removed_ref[span, 0], removed_ref[span, 1]
+    for span in range(removed_ref.shape[1]):
+        first, last = removed_ref[0, span], removed_ref[1, span]
         gone = gone + (last - first)
         for b in range(local_blocks):
             block = first_block + b
@@ -53,6 +53,7 @@
 
 
 code_limit = 32767.0
+exponent_scale = score_scale * 1.4426950408889634
 tiny_peak = 1e-30
 nt_dims = (((1,), (1,)), ((), ()))
 tn_dims = (((0,), (0,)), ((), ()))
@@ -64,20 +65,18 @@
     scores = (
         lax.dot_general(latents, q, nt_dims, preferred_element_type=jnp.float32)
         + lax.dot_general(keys, qr, nt_dims, preferred_element_type=jnp.float32)
-    ) * score_scale
-    lifted, sums, weights = [], [], []
+    )
+    lifted, weights = [], []
     for b in range(blocks):
         part = scores[b * block_rows : (b + 1) * block_rows]
         block_max = jnp.max(part, axis=0, keepdims=True)
-        weights.append(jnp.exp(part - block_max).astype(jnp.bfloat16))
-        sums.append(jnp.sum(weights[b].astype(jnp.float32), axis=0, keepdims=True))
-        lifted.append(jnp.where(inside[b] == 0, block_max, floor_value))
+        weights.append(jnp.exp2((part - block_max) * exponent_scale).astype(jnp.bfloat16))
+        lifted.append(jnp.where(inside[b] == 0, block_max * score_scale, floor_value))
     top = lifted[0]
     for b in range(1, blocks):
         top = jnp.maximum(top, lifted[b])
     factors = [jnp.where(inside[b] == 0, jnp.exp(lifted[b] - top), 0.0) for b in range(blocks)]
-    total = sum(sums[b] * factors[b] for b in range(blocks))
-    return top, total, weights, factors
+    return top, weights, factors
 
 
 def weighted(columns, weights, factors):
@@ -145,8 +144,20 @@
     def index_of(place_id, pair_id, core_id):
         return (place_id * 2 + pair_id) * 2 + core_id
 
+    bits = far.bit_length() - 1
+
+    def flipped(bit):
+        return (1 - place // 2**bit % 2 * 2) * 2**bit
+
     def place_at(step):
-        return (place + 1 + step) % far
+        apart = far - 1 - step
+        return place + sum(flipped(bit) * (apart // 2**bit % 2) for bit in range(bits))
+
+    def next_place(step):
+        apart = far - 1 - step
+        return place + sum(
+            flipped(bit) * jnp.where(apart % 2 ** (bit + 1) == 2**bit, 1, 0) for bit in range(bits)
+        )
 
     def chip_at(step):
         pair_id = (pair + 1 + step // far) % 2
@@ -166,18 +177,18 @@
     for other in [sibling, partner]:
         pl.semaphore_signal(barrier, 1, device_id={"ctx": other})
 
-    def greet(step, nothing):
-        pl.semaphore_signal(barrier, 1, device_id={"ctx": index_of(place_at(step), pair, core)})
-        return nothing
-
-    lax.fori_loop(0, far - 1, greet, 0)
+    for bit in range(bits):
+        other = index_of(place + flipped(bit), pair, core)
+        pl.semaphore_signal(barrier, 1, device_id={"ctx": other})
     blocks, block_rows = lat_ref.shape[:2]
     tokens, rope_width = new_rope_ref.shape
     halves, group = rope_width // 2, 128 // rope_width
     slabs = tokens // group
     turned = lat_ref[...].reshape(columns.shape[2], lat_width).T
-    columns[0] = turned[:width]
-    columns[1] = turned[width:]
+    columns[0, :width] = turned[:width]
+    columns[1, :width] = turned[width:]
+    for side in range(2):
+        columns[side, width:] = jnp.ones((16, columns.shape[2]), jnp.bfloat16)
     inside, drops, kept_rows = span_scalars(
         removed_ref, me * blocks, blocks, blocks * 4 * far, block_rows
     )
@@ -238,7 +249,7 @@
         own_lanes = lane // rope_width == row % tokens % group
         return jnp.where(own_lanes, rows, 0.0).astype(jnp.bfloat16)
 
-    pl.semaphore_wait(barrier, far + 1)
+    pl.semaphore_wait(barrier, bits + 2)
 
     def copies(source, landing, source_meta, landing_meta, sems, slot, target):
         return [
@@ -259,7 +270,7 @@
         return copies(pair_out, pair_in, pair_out_meta, pair_in_meta, pair_sems, slot, partner)
 
     def far_copies(slot):
-        target = index_of(place_at(slot), pair, core)
+        target = index_of(next_place(slot), pair, core)
         return copies(far_out, far_in, far_out_meta, far_in_meta, far_sems, slot, target)
 
     def start(both):
@@ -270,27 +281,45 @@
         for copy in both:
             copy.wait_recv()
 
+    def put_held(state, slot):
+        held_rows[slot, 0:1] = state[0]
+        held_rows[slot, 1:2] = state[1]
+        held_acc[slot] = state[2]
+
+    def get_held(slot):
+        return held_rows[slot, 0:1], held_rows[slot, 1:2], held_acc[slot]
+
     def with_sibling(slot):
-        state = held_rows[slot, 0:1], held_rows[slot, 1:2], held_acc[slot]
         landed(core_copies(slot))
-        return merge(state, get_state(core_in, core_in_meta, slot))
-
-    def gathered(step):
+        return merge(get_held(slot), get_state(core_in, core_in_meta, slot))
+
+    def gather(step):
         state = with_sibling(far + step)
         landed(pair_copies(step))
-        return merge(state, get_state(pair_in, pair_in_meta, step))
+        put_held(merge(state, get_state(pair_in, pair_in_meta, step)), far + step)
+        for bit in range(bits):
+
+            @pl.when((far - 1 - step) % 2 ** (bit + 1) == 0)
+            def take_far():
+                landed(far_copies(step - 2**bit))
+                arrived = get_state(far_in, far_in_meta, step - 2**bit)
+                put_held(merge(get_held(far + step), arrived), far + step)
+
+    def to_far(step):
+        gather(step)
+        put_state(get_held(far + step), far_out, far_out_meta, step)
+        start(far_copies(step))
 
     def chip_step(step, nothing):
         q_copy(step).wait()
-        top, total, weights, factors = block_weights(
+        top, weights, factors = block_weights(
             q_buf[step], rope_rows(chip_at(step)), lat_ref, key_rows[...], inside
         )
         theirs = weighted(columns[1 - core], weights, factors)
-        put_state((top, total, theirs), core_out, core_out_meta, step)
+        total = theirs[width : width + 1]
+        put_state((top, total, theirs[:width]), core_out, core_out_meta, step)
         start(core_copies(step))
-        held_rows[step, 0:1] = top
-        held_rows[step, 1:2] = total
-        held_acc[step] = weighted(columns[core], weights, factors)
+        put_held((top, total, weighted(columns[core, :width], weights, factors)), step)
 
         @pl.when((step >= 1) & (step <= far))
         def to_pair():
@@ -298,9 +327,8 @@
             start(pair_copies(step - 1))
 
         @pl.when(step > far)
-        def to_far():
-            put_state(gathered(step - 1 - far), far_out, far_out_meta, step - 1 - far)
-            start(far_copies(step - 1 - far))
+        def onward():
+            to_far(step - 1 - far)
 
         return nothing
 
@@ -310,13 +338,9 @@
     fresh = new_state(
         q_buf[last], rope_rows(chip_at(last)), new_lat_ref[...], half, new_keys[...]
     )
-    state = merge(gathered(far - 1), fresh)
-
-    def take_far(step, carried):
-        landed(far_copies(step))
-        return merge(carried, get_state(far_in, far_in_meta, step))
-
-    top, total, acc = lax.fori_loop(0, far - 1, take_far, state)
+    gather(far - 1)
+
+    top, total, acc = merge(get_held(last), fresh)
     done = acc / total
     spare = -done.shape[1] % 128
     if spare:
@@ -382,7 +406,7 @@
         out_specs=vmem,
         scratch_shapes=room(2 * far) + room(far) + room(far - 1) + [
             pltpu.VMEM((2 * far, chip_rows, lat_width), jnp.bfloat16),
-            pltpu.VMEM((2, width, keys), jnp.bfloat16),
+            pltpu.VMEM((2, width + 16, keys), jnp.bfloat16),
             pltpu.VMEM((2 * far, width, chip_rows), jnp.float32),
             pltpu.VMEM((2 * far, 8, chip_rows), jnp.float32),
             pltpu.VMEM((own_count, width), jnp.bfloat16),
@@ -409,7 +433,7 @@
     )(
         q_latent.reshape(chips, chip_rows, lat_width),
         q_rope.reshape(chips, 2 * own_heads, tokens * rope_width),
-        cache_latent, cache_rope, new_latent, new_rope, removed,
+        cache_latent, cache_rope, new_latent, new_rope, removed.T,
         jnp.asarray(rope_tables(rope_width)),
     )
     return attended.reshape(own_heads, tokens, lat_width)

time: 40.5 us -> 38.9 us (0.960)
  local copies, waits for them, and re-layouts: 2.97 us -> 1.62 us
    unnamed x2 -> x1, local copies, waits for them, and re-layouts: 2.97 us -> 1.62 us
where the time goes in v5:
time: 38.9 us; the launch traced here: 38.8 us
  Pallas kernels  37.1 us (95%)
  local copies, waits for them, and re-layouts  1.62 us (4%)
    pallas_call x1, Pallas kernels, shards(): pl.pallas_call(lambda *refs: exchange_kernel(far, *refs), out_shape=jax.S...  37.1 us
    unnamed x1, local copies, waits for them, and re-layouts  1.62 us

profile of v5, /device:TPU:0, one launch (start us, length us, event | category | flops | bytes accessed | tf_op | source)
XLA Modules:
  0.0 38.8 jit_solution(13466568012915574883)
XLA Ops:
  0.0 37.1 %shard_map.82 = bf16[192,512]{1,0:T(8,128)(2,1)} custom-call(bf16[8,384,512]{2,1,0:T(8,128)(2,1)} %bitcast.5, bf16[8,16,1536]{2,1,0:T(8,128)(2,1)} %bitcast.6, bf16[4,128,512]{2,1,0:T(8,128)(2,1)} %refs_2_.1, bf16[4,64,128]{2,1,0:T(8,128)(2,1)} %refs_3_.1, bf16[24,512]{1,0:T(8,128)(2,1)} %refs_4_.1, bf16[24,64]{1,0:T(8,128)(2,1)} %refs_5_.1, ...), custom_call_target="tpu_custom_call" | custom-call | flops 3422552064 | bytes 4128768 | tf_op jit(solution)/shard_map/pallas_call | solution.py:400
  37.1 1.6 %copy.10 = bf16[8,24,512]{2,1,0:T(8,128)(2,1)} copy(bf16[8,24,512]{2,1,0:T(8,128)(2,1)} %bitcast.4) | data formatting | bytes 393216

commit v6 on v5

--- a/solution.py
+++ b/solution.py
@@ -168,9 +168,10 @@
 
     def fetch(step, nothing):
         q_copy(step).start()
+        q_copy(far + step).start()
         return nothing
 
-    lax.fori_loop(0, 2 * far, fetch, 0)
+    lax.fori_loop(0, far, fetch, 0)
     sibling = index_of(place, pair, 1 - core)
     partner = index_of(place, 1 - pair, core)
     barrier = pltpu.get_barrier_semaphore()
@@ -310,7 +311,7 @@
         put_state(get_held(far + step), far_out, far_out_meta, step)
         start(far_copies(step))
 
-    def chip_step(step, nothing):
+    def chip_step(step):
         q_copy(step).wait()
         top, weights, factors = block_weights(
             q_buf[step], rope_rows(chip_at(step)), lat_ref, key_rows[...], inside
@@ -321,18 +322,24 @@
         start(core_copies(step))
         put_held((top, total, weighted(columns[core, :width], weights, factors)), step)
 
-        @pl.when((step >= 1) & (step <= far))
-        def to_pair():
-            put_state(with_sibling(step - 1), pair_out, pair_out_meta, step - 1)
-            start(pair_copies(step - 1))
-
-        @pl.when(step > far)
+    chip_step(0)
+
+    def round_of(step, nothing):
+        @pl.when(step < far - 1)
+        def ahead():
+            chip_step(step + 1)
+
+        put_state(with_sibling(step), pair_out, pair_out_meta, step)
+        start(pair_copies(step))
+
+        @pl.when(step >= 1)
         def onward():
-            to_far(step - 1 - far)
-
+            to_far(step - 1)
+
+        chip_step(far + step)
         return nothing
 
-    lax.fori_loop(0, 2 * far, chip_step, 0)
+    lax.fori_loop(0, far, round_of, 0)
     last = 2 * far - 1
     half = jnp.where(core == 0, new_lat_ref[:, :width], new_lat_ref[:, width:])
     fresh = new_state(
@@ -423,7 +430,7 @@
             pltpu.SemaphoreType.DMA((2,)),
         ],
         compiler_params=pltpu.CompilerParams(
-            collective_id=0, has_side_effects=True, vmem_limit_bytes=60 * 1024 * 1024
+            collective_id=0, has_side_effects=True, vmem_limit_bytes=53 * 1024 * 1024
         ),
         cost_estimate=pl.CostEstimate(
             flops=2 * rows * keys * (2 * lat_width + rope_width),

time: 38.9 us -> 41.9 us (1.077)
  local copies, waits for them, and re-layouts: 1.62 us -> 5.35 us
  Pallas kernels: 37.1 us -> 36.1 us
    unnamed x1 -> x13, local copies, waits for them, and re-layouts: 1.62 us -> 5.35 us
    pallas_call x1, Pallas kernels: 37.1 us -> 36.1 us  [shards(): pl.pallas_call(lambda *refs: exchange_kernel(far, *refs), out_shape=jax.S...]
where the time goes in v6:
time: 41.9 us; the launch traced here: 41.5 us
  Pallas kernels  36.1 us (86%)
  local copies, waits for them, and re-layouts  5.35 us (13%)
    pallas_call x1, Pallas kernels, shards(): pl.pallas_call(lambda *refs: exchange_kernel(far, *refs), out_shape=jax.S...  36.1 us
    unnamed x13, local copies, waits for them, and re-layouts  5.35 us

profile of v6, /device:TPU:0, one launch (start us, length us, event | category | flops | bytes accessed | tf_op | source)
XLA Modules:
  0.0 41.5 jit_solution(6496961075830884860)
XLA Ops:
  0.0 0.0 copy-start
  0.0 1.0 %copy-done = bf16[128,1536]{1,0:T(8,128)(2,1)S(1)} copy-done((bf16[128,1536]{1,0:T(8,128)(2,1)S(1)}, bf16[128,1536]{1,0:T(8,128)(2,1)}, u32[]{:S(2)}) %copy-start) | copy-done | bytes 393240
  1.0 0.0 copy-start.1
  1.0 0.8 %copy-done.1 = bf16[4,64,128]{2,1,0:T(8,128)(2,1)S(1)} copy-done((bf16[4,64,128]{2,1,0:T(8,128)(2,1)S(1)}, bf16[4,64,128]{2,1,0:T(8,128)(2,1)}, u32[]{:S(2)}) %copy-start.1) | copy-done | bytes 65560
  1.8 0.0 copy-start.2
  1.8 0.7 %copy-done.2 = bf16[24,512]{1,0:T(8,128)(2,1)S(1)} copy-done((bf16[24,512]{1,0:T(8,128)(2,1)S(1)}, bf16[24,512]{1,0:T(8,128)(2,1)}, u32[]{:S(2)}) %copy-start.2) | copy-done | bytes 24600
  2.6 0.0 copy-start.3
  2.6 0.7 %copy-done.3 = bf16[24,64]{1,0:T(8,128)(2,1)S(1)} copy-done((bf16[24,64]{1,0:T(8,128)(2,1)S(1)}, bf16[24,64]{1,0:T(8,128)(2,1)}, u32[]{:S(2)}) %copy-start.3) | copy-done | bytes 3096
  3.3 0.0 copy-start.4
  3.3 0.7 %copy-done.4 = s32[12,2]{0,1:T(2,128)S(1)} copy-done((s32[12,2]{0,1:T(2,128)S(1)}, s32[12,2]{0,1:T(2,128)}, u32[]{:S(2)}) %copy-start.4) | copy-done | bytes 120
  3.9 0.0 copy-start.5
  3.9 0.7 %copy-done.5 = f32[40,128]{1,0:T(8,128)S(1)} copy-done((f32[40,128]{1,0:T(8,128)S(1)}, f32[40,128]{1,0:T(8,128)}, u32[]{:S(2)}) %copy-start.5) | copy-done | bytes 20504
  4.7 36.1 %shard_map.82 = bf16[192,512]{1,0:T(8,128)(2,1)S(1)} custom-call(bf16[8,384,512]{2,1,0:T(8,128)(2,1)} %bitcast.7, bf16[8,16,1536]{2,1,0:T(8,128)(2,1)S(1)} %bitcast.5, bf16[4,128,512]{2,1,0:T(8,128)(2,1)} %refs_2_.1, bf16[4,64,128]{2,1,0:T(8,128)(2,1)S(1)} %copy-done.1, bf16[24,512]{1,0:T(8,128)(2,1)S(1)} %copy-done.2, bf16[24,64]{1,0:T(8,128)(2,1)S(1)} %copy-done.3, ...), custom_call_target="tpu_custom_call" | custom-call | flops 3422552064 | bytes 4128768 | tf_op jit(solution)/shard_map/pallas_call | solution.py:407
  40.8 0.7 %copy.10 = bf16[8,24,512]{2,1,0:T(8,128)(2,1)} copy(bf16[8,24,512]{2,1,0:T(8,128)(2,1)S(1)} %bitcast.4) | data formatting | bytes 393216
Async XLA Ops:
  0.0 1.0 %copy-start = (bf16[128,1536]{1,0:T(8,128)(2,1)S(1)}, bf16[128,1536]{1,0:T(8,128)(2,1)}, u32[]{:S(2)}) copy-start(bf16[128,1536]{1,0:T(8,128)(2,1)} %param.9) | copy-start | bytes 1179652
  1.0 0.8 %copy-start.1 = (bf16[4,64,128]{2,1,0:T(8,128)(2,1)S(1)}, bf16[4,64,128]{2,1,0:T(8,128)(2,1)}, u32[]{:S(2)}) copy-start(bf16[4,64,128]{2,1,0:T(8,128)(2,1)} %refs_3_.1) | copy-start | bytes 196612
  1.8 0.7 %copy-start.2 = (bf16[24,512]{1,0:T(8,128)(2,1)S(1)}, bf16[24,512]{1,0:T(8,128)(2,1)}, u32[]{:S(2)}) copy-start(bf16[24,512]{1,0:T(8,128)(2,1)} %refs_4_.1) | copy-start | bytes 73732
  2.6 0.7 %copy-start.3 = (bf16[24,64]{1,0:T(8,128)(2,1)S(1)}, bf16[24,64]{1,0:T(8,128)(2,1)}, u32[]{:S(2)}) copy-start(bf16[24,64]{1,0:T(8,128)(2,1)} %refs_5_.1) | copy-start | bytes 9220
  3.3 0.7 %copy-start.4 = (s32[12,2]{0,1:T(2,128)S(1)}, s32[12,2]{0,1:T(2,128)}, u32[]{:S(2)}) copy-start(s32[12,2]{0,1:T(2,128)} %param.14) | copy-start | bytes 292
  3.9 0.7 %copy-start.5 = (f32[40,128]{1,0:T(8,128)S(1)}, f32[40,128]{1,0:T(8,128)}, u32[]{:S(2)}) copy-start(f32[40,128]{1,0:T(8,128)} %constant.2.clone.refs_7_) | copy-start | bytes 61444

commit v7 on v6

--- a/solution.py
+++ b/solution.py
@@ -133,7 +133,7 @@
     pair_out, pair_in, pair_out_meta, pair_in_meta,
     far_out, far_in, far_out_meta, far_in_meta,
     q_buf, columns, held_acc, held_rows, swap_out, swap_in,
-    key_rows, new_keys, slab_cos, slab_sin, pick,
+    key_rows, slab_cos, slab_sin, pick,
     core_sems, pair_sems, far_sems, q_sems, swap_sems,
 ):
     own, lat_width = out_ref.shape
@@ -205,11 +205,6 @@
     angles = angles_of(kept_rows + row * group + lane // rope_width, *along)
     slab_cos[...] = jnp.cos(angles)
     slab_sin[...] = signed(jnp.sin(angles))
-    angles = angles_of(kept_rows + lax.broadcasted_iota(jnp.int32, (tokens, 128), 0), *along)
-    fresh_rope = jnp.concatenate([new_rope_ref[...].astype(jnp.float32)] * group, axis=1)
-    new_keys[...] = turn_slab(
-        fresh_rope, jnp.cos(angles), signed(jnp.sin(angles)), rope_width
-    ).astype(jnp.bfloat16)
     lane = lax.broadcasted_iota(jnp.int32, (halves, 128), 1)
     dropped = jnp.zeros((halves, 128), jnp.int32)
     for b in range(blocks):
@@ -342,8 +337,13 @@
     lax.fori_loop(0, far, round_of, 0)
     last = 2 * far - 1
     half = jnp.where(core == 0, new_lat_ref[:, :width], new_lat_ref[:, width:])
+    angles = angles_of(kept_rows + lax.broadcasted_iota(jnp.int32, (tokens, 128), 0), *along)
+    fresh_rope = jnp.concatenate([new_rope_ref[...].astype(jnp.float32)] * group, axis=1)
+    fresh_keys = turn_slab(
+        fresh_rope, jnp.cos(angles), signed(jnp.sin(angles)), rope_width
+    ).astype(jnp.bfloat16)
     fresh = new_state(
-        q_buf[last], rope_rows(chip_at(last)), new_lat_ref[...], half, new_keys[...]
+        q_buf[last], rope_rows(chip_at(last)), new_lat_ref[...], half, fresh_keys
     )
     gather(far - 1)
 
@@ -419,7 +419,6 @@
             pltpu.VMEM((own_count, width), jnp.bfloat16),
             pltpu.VMEM((own_count, width), jnp.bfloat16),
             pltpu.VMEM((keys, 128), jnp.bfloat16),
-            pltpu.VMEM((tokens, 128), jnp.bfloat16),
             pltpu.VMEM((slabs, 128), jnp.float32),
             pltpu.VMEM((slabs, 128), jnp.float32),
             pltpu.VMEM((chip_rows, slabs * head_rows), jnp.bfloat16),
@@ -430,7 +429,7 @@
             pltpu.SemaphoreType.DMA((2,)),
         ],
         compiler_params=pltpu.CompilerParams(
-            collective_id=0, has_side_effects=True, vmem_limit_bytes=53 * 1024 * 1024
+            collective_id=0, has_side_effects=True, vmem_limit_bytes=60 * 1024 * 1024
         ),
         cost_estimate=pl.CostEstimate(
             flops=2 * rows * keys * (2 * lat_width + rope_width),

time: 41.9 us -> 38.8 us (0.926)
  local copies, waits for them, and re-layouts: 5.35 us -> 1.62 us
  Pallas kernels: 36.1 us -> 37 us
    unnamed x13 -> x1, local copies, waits for them, and re-layouts: 5.35 us -> 1.62 us
    pallas_call x1, Pallas kernels: 36.1 us -> 37 us  [shards(): pl.pallas_call(lambda *refs: exchange_kernel(far, *refs), out_shape=jax.S...]
where the time goes in v7:
time: 38.8 us; the launch traced here: 38.6 us
  Pallas kernels  37 us (95%)
  local copies, waits for them, and re-layouts  1.62 us (4%)
    pallas_call x1, Pallas kernels, shards(): pl.pallas_call(lambda *refs: exchange_kernel(far, *refs), out_shape=jax.S...  37 us
    unnamed x1, local copies, waits for them, and re-layouts  1.62 us

profile of v7, /device:TPU:0, one launch (start us, length us, event | category | flops | bytes accessed | tf_op | source)
XLA Modules:
  0.0 38.6 jit_solution(4085894987570022573)
XLA Ops:
  0.0 37.0 %shard_map.82 = bf16[192,512]{1,0:T(8,128)(2,1)} custom-call(bf16[8,384,512]{2,1,0:T(8,128)(2,1)} %bitcast.5, bf16[8,16,1536]{2,1,0:T(8,128)(2,1)} %bitcast.6, bf16[4,128,512]{2,1,0:T(8,128)(2,1)} %refs_2_.1, bf16[4,64,128]{2,1,0:T(8,128)(2,1)} %refs_3_.1, bf16[24,512]{1,0:T(8,128)(2,1)} %refs_4_.1, bf16[24,64]{1,0:T(8,128)(2,1)} %refs_5_.1, ...), custom_call_target="tpu_custom_call" | custom-call | flops 3422552064 | bytes 4128768 | tf_op jit(solution)/shard_map/pallas_call | solution.py:407
  37.0 1.6 %copy.10 = bf16[8,24,512]{2,1,0:T(8,128)(2,1)} copy(bf16[8,24,512]{2,1,0:T(8,128)(2,1)} %bitcast.4) | data formatting | bytes 393216
